TPU v7x, 128 devices: a whole 4x4x4 slice. The times are simulated.
128 devices in a mesh: section: 8 (over x_hi, z), dp: 16 (over y, x_lo, core).
Axes of the slice: x: 4 (x_hi: 2, x_lo: 2; x = x_hi * 2 + x_lo), y: 4, z: 4, core: 2. Of those that a mesh axis runs over, the one named last changes fastest.
Arguments:
- hidden_states: bfloat16 [8, 2, 2048, 8192], P('section', None, 'dp'), may hold values from -12 to 12
- key_rows: bfloat16 [8, 2, 2048, 4096], P('section', None, 'dp'), may hold values from -27 to 27
- value_rows: bfloat16 [8, 2, 2048, 4096], P('section', None, 'dp'), may hold values from -6 to 6
- latents: bfloat16 [2, 2048, 768], P(None, 'dp'), may hold values from -6 to 6
- next_latents: bfloat16 [2048, 768], P('dp'), may hold values from -6 to 6
- media_index: int32 [2, 2048], P(None, 'dp'), may hold values from 0 to 1
- cotangent: bfloat16 [2, 2048, 8192], P(None, 'dp'), may hold values from -6 to 6
- gate_alpha: float32 [8], P('section'), may hold values from 0.3 to 1.2
- weights: float32 [8, 2, 768, 4096], P('section', None, None, 'dp'), may hold values from -0.21875 to 0.21875
- moment_first: float32 [8, 2, 768, 4096], P('section', None, None, 'dp'), may hold values from -4 to 4
- moment_second: float32 [8, 2, 768, 4096], P('section', None, None, 'dp'), may hold values from 0.1 to 10
Outputs:
- input_grads: bfloat16 [8, 2, 2048, 8192], P('section', None, 'dp')
- new_weights: float32 [8, 2, 768, 4096], P('section', None, None, 'dp')
- next_keyvals: bfloat16 [8, 2, 2048, 4096], P('section', None, 'dp')
Inputs may be any that keep to these rules, and one draw needn't show every extreme that they name: `media_index`: each token attends to one of the 2 media items held with its own block of 128 tokens.
All inputs are finite; a program needn't handle non-finite values.
Results may differ from a plain program's by a relative error of at most 0.0085.
Values may be sent and summed in bfloat16 or wider, within the bound.
A program may use at most 192 MiB of HBM per device.

v0:
```python
import math

import jax
import jax.numpy as jnp
from jax import lax
from jax.sharding import PartitionSpec as P

HEADS = 32
HEAD_DIM = 128
LATENTS = 64


def shifted(value, axis, steps):
    count = lax.axis_size(axis)
    first, last = (max(0, -steps), min(count, count - steps))
    return lax.ppermute(value, axis, [(source, source + steps) for source in range(first, last)])


def attend_back(states, media_ids, upstream, key_block, value_block, gate_tanh):
    count = states.shape[0]
    rows_here = key_block.shape[0]
    span = key_block.shape[1]
    width = states.shape[1]
    scale = 1.0 / math.sqrt(HEAD_DIM)
    floats = states.astype(jnp.float32)
    root_mean = jnp.sqrt(jnp.mean(floats * floats, axis=1, keepdims=True) + 1e-06)
    normed = floats / root_mean
    query = normed[:, :span].astype(jnp.bfloat16).reshape(count, HEADS, HEAD_DIM)
    key_heads = key_block.reshape(rows_here, HEADS, HEAD_DIM)
    value_heads = value_block.reshape(rows_here, HEADS, HEAD_DIM)
    scores = (
        jnp.einsum("thd,rhd->htr", query, key_heads, preferred_element_type=jnp.float32) * scale
    )
    allowed = (jnp.arange(rows_here) // LATENTS)[None, :] == media_ids[:, None]
    scores = jnp.where(allowed[None], scores, -1e30)
    peak = jnp.max(scores, axis=2, keepdims=True)
    raised = jnp.exp(scores - peak)
    probs = raised / jnp.sum(raised, axis=2, keepdims=True)
    probs_low = probs.astype(jnp.bfloat16)
    grad_out = (gate_tanh * upstream[:, :span].astype(jnp.float32)).astype(jnp.bfloat16)
    grad_out = grad_out.reshape(count, HEADS, HEAD_DIM)
    grad_probs = jnp.einsum(
        "thd,rhd->htr", grad_out, value_heads, preferred_element_type=jnp.float32
    )
    weighted = jnp.sum(probs * grad_probs, axis=2, keepdims=True)
    grad_scores = (probs * (grad_probs - weighted)).astype(jnp.bfloat16)
    grad_query = (
        jnp.einsum("htr,rhd->thd", grad_scores, key_heads, preferred_element_type=jnp.float32)
        * scale
    )
    grad_keys = (
        jnp.einsum("htr,thd->rhd", grad_scores, query, preferred_element_type=jnp.float32) * scale
    ).astype(jnp.bfloat16)
    grad_values = jnp.einsum(
        "htr,thd->rhd", probs_low, grad_out, preferred_element_type=jnp.float32
    ).astype(jnp.bfloat16)
    grad_normed = jnp.pad(grad_query.reshape(count, span), ((0, 0), (0, width - span)))
    inner = jnp.mean(grad_normed * normed, axis=1, keepdims=True)
    grad_input = upstream.astype(jnp.float32) + (grad_normed - normed * inner) / root_mean
    return (
        grad_input.astype(jnp.bfloat16),
        grad_keys.reshape(rows_here, span),
        grad_values.reshape(rows_here, span),
    )


def pick_slot(array, slot):
    return lax.dynamic_index_in_dim(array, slot, 0, keepdims=False)


def body(
    hidden_states,
    key_rows,
    value_rows,
    latents,
    next_latents,
    media_index,
    cotangent,
    gate_alpha,
    weights,
    moment_first,
    moment_second,
):
    sections = lax.axis_size("section")
    place = lax.axis_index("section")
    states_all = hidden_states[0]
    keys_all = key_rows[0]
    values_all = value_rows[0]
    gate_tanh = jnp.tanh(gate_alpha[0])
    micro = states_all.shape[0]
    span = keys_all.shape[2]
    lat_width = latents.shape[2]
    ticks = micro + sections - 1

    def advance(carry, tick):
        incoming, grad_buffer, stored = carry
        which = tick - (sections - 1 - place)
        valid = (which >= 0) & (which < micro)
        slot = jnp.clip(which, 0, micro - 1)
        upstream = jnp.where(place == sections - 1, pick_slot(cotangent, slot), incoming)
        grad_x, grad_k, grad_v = attend_back(
            pick_slot(states_all, slot),
            pick_slot(media_index, slot),
            upstream,
            pick_slot(keys_all, slot),
            pick_slot(values_all, slot),
            gate_tanh,
        )
        grad_buffer = jnp.where(
            valid, lax.dynamic_update_index_in_dim(grad_buffer, grad_x, slot, 0), grad_buffer
        )

        def add_term(total):
            paired = jnp.stack([grad_k, grad_v])
            return total + jnp.einsum(
                "rl,irc->ilc", pick_slot(latents, slot), paired, preferred_element_type=jnp.float32
            )

        stored = lax.cond(valid, add_term, lambda total: total, stored)
        return ((incoming, grad_buffer, stored), grad_x)

    stored_init = jnp.zeros((2, lat_width, span), jnp.float32)
    start = (
        jnp.zeros(states_all.shape[1:], jnp.bfloat16),
        jnp.zeros(states_all.shape, jnp.bfloat16),
        stored_init,
    )

    def tick_step(carry, tick):
        carry, grad_x = advance(carry, tick)
        incoming = shifted(grad_x, "section", -1)
        return ((incoming, carry[1], carry[2]), None)

    carry, unused = lax.scan(tick_step, start, jnp.arange(ticks - 1))
    carry, unused_last = advance(carry, ticks - 1)
    grad_buffer = carry[1]
    grads = lax.psum_scatter(
        carry[2].astype(jnp.bfloat16), "dp", scatter_dimension=2, tiled=True
    ).astype(jnp.float32)
    current = weights[0]
    first = 0.9 * moment_first[0] + 0.1 * grads
    second = 0.95 * moment_second[0] + 0.05 * grads * grads
    updated = current - 0.02 * (first / (jnp.sqrt(second) + 1e-08) + 0.1 * current)
    weights_low = updated.astype(jnp.bfloat16)
    keyvals = jnp.einsum(
        "rl,ilc->irc",
        next_latents,
        lax.all_gather(weights_low, "dp", axis=2, tiled=True),
        preferred_element_type=jnp.float32,
    ).astype(jnp.bfloat16)
    return (grad_buffer[None], updated[None], keyvals[None])


def solution(mesh):
    in_specs = (
        P("section", None, "dp", None),
        P("section", None, "dp", None),
        P("section", None, "dp", None),
        P(None, "dp", None),
        P("dp", None),
        P(None, "dp"),
        P(None, "dp", None),
        P("section"),
        P("section", None, None, "dp"),
        P("section", None, None, "dp"),
        P("section", None, None, "dp"),
    )
    out_specs = (
        P("section", None, "dp", None),
        P("section", None, None, "dp"),
        P("section", None, "dp", None),
    )
    return jax.shard_map(body, mesh=mesh, in_specs=in_specs, out_specs=out_specs, check_vma=False)
```

profile of v0, /device:TPU:0, one launch (start us, length us, event | category | flops | bytes accessed | tf_op | source)
XLA Modules:
  0.0 996.2 jit_solution(2465727027657491830)
XLA Ops:
  7.8 4.1 copy.48
  11.8 6.5 copy.49
  30.6 3.0 constant_dynamic-slice_fusion.4
  37.7 9.9 broadcast_in_dim.75
  47.6 667.0 %while.22 = (s32[]{:T(128)}, bf16[128,8192]{0,1:T(8,128)(2,1)}, bf16[2,128,8192]{1,2,0:T(8,128)(2,1)}, f32[2,768,4096]{1,2,0:T(8,128)}, pred[]{:T(512)}, /*index...) while((s32[]{:T(128)}, bf16[128,8192]{0,1:T(8,128)(2,1)}, ...), condition=%wide.region_8.9_spmd, body=%wide.region_0.8_spmd.sunk | while | flops 2320512256 | bytes 161817072 | solution.py:134
  55.7 3.8 convert_divide_fusion.3
  59.6 2.7 constant_dynamic-slice_fusion.10
  75.9 6.3 fusion.117
  85.6 2.8 fusion.119
  88.4 43.7 %collective-permute-done = bf16[128,8192]{0,1:T(8,128)(2,1)} collective-permute-done((bf16[128,8192]{0,1:T(8,128)(2,1)}, bf16[128,8192]{0,1:T(8,128)(2,1)}, u32[]{:S(2)}, u32[]{:S(2)}) %collective-permute-start) | collective-permute-done | bytes 2097184 | tf_op jit(solution)/shard_map/while/body/eval_jaxpr/ppermute | solution.py:16
  140.2 3.8 convert_divide_fusion.3
  144.1 2.7 constant_dynamic-slice_fusion.10
  160.3 6.3 fusion.117
  170.0 2.8 fusion.119
  172.8 42.9 %collective-permute-done = bf16[128,8192]{0,1:T(8,128)(2,1)} collective-permute-done((bf16[128,8192]{0,1:T(8,128)(2,1)}, bf16[128,8192]{0,1:T(8,128)(2,1)}, u32[]{:S(2)}, u32[]{:S(2)}) %collective-permute-start) | collective-permute-done | bytes 2097184 | tf_op jit(solution)/shard_map/while/body/eval_jaxpr/ppermute | solution.py:16
  223.9 3.8 convert_divide_fusion.3
  227.8 2.7 constant_dynamic-slice_fusion.10
  244.0 6.3 fusion.117
  253.7 2.8 fusion.119
  256.5 42.0 %collective-permute-done = bf16[128,8192]{0,1:T(8,128)(2,1)} collective-permute-done((bf16[128,8192]{0,1:T(8,128)(2,1)}, bf16[128,8192]{0,1:T(8,128)(2,1)}, u32[]{:S(2)}, u32[]{:S(2)}) %collective-permute-start) | collective-permute-done | bytes 2097184 | tf_op jit(solution)/shard_map/while/body/eval_jaxpr/ppermute | solution.py:16
  306.6 3.8 convert_divide_fusion.3
  310.5 2.7 constant_dynamic-slice_fusion.10
  326.8 6.3 fusion.117
  336.5 2.8 fusion.119
  339.3 44.4 %collective-permute-done = bf16[128,8192]{0,1:T(8,128)(2,1)} collective-permute-done((bf16[128,8192]{0,1:T(8,128)(2,1)}, bf16[128,8192]{0,1:T(8,128)(2,1)}, u32[]{:S(2)}, u32[]{:S(2)}) %collective-permute-start) | collective-permute-done | bytes 2097184 | tf_op jit(solution)/shard_map/while/body/eval_jaxpr/ppermute | solution.py:16
  391.8 3.8 convert_divide_fusion.3
  395.7 2.7 constant_dynamic-slice_fusion.10
  411.9 6.3 fusion.117
  421.6 2.8 fusion.119
  424.4 43.4 %collective-permute-done = bf16[128,8192]{0,1:T(8,128)(2,1)} collective-permute-done((bf16[128,8192]{0,1:T(8,128)(2,1)}, bf16[128,8192]{0,1:T(8,128)(2,1)}, u32[]{:S(2)}, u32[]{:S(2)}) %collective-permute-start) | collective-permute-done | bytes 2097184 | tf_op jit(solution)/shard_map/while/body/eval_jaxpr/ppermute | solution.py:16
  475.9 3.8 convert_divide_fusion.3
  479.8 2.7 constant_dynamic-slice_fusion.10
  496.1 6.3 fusion.117
  505.8 2.8 fusion.119
  508.6 42.5 %collective-permute-done = bf16[128,8192]{0,1:T(8,128)(2,1)} collective-permute-done((bf16[128,8192]{0,1:T(8,128)(2,1)}, bf16[128,8192]{0,1:T(8,128)(2,1)}, u32[]{:S(2)}, u32[]{:S(2)}) %collective-permute-start) | collective-permute-done | bytes 2097184 | tf_op jit(solution)/shard_map/while/body/eval_jaxpr/ppermute | solution.py:16
  559.1 3.8 convert_divide_fusion.3
  563.1 2.7 constant_dynamic-slice_fusion.10
  579.3 6.3 fusion.117
  589.0 2.8 fusion.119
  591.8 41.5 %collective-permute-done = bf16[128,8192]{0,1:T(8,128)(2,1)} collective-permute-done((bf16[128,8192]{0,1:T(8,128)(2,1)}, bf16[128,8192]{0,1:T(8,128)(2,1)}, u32[]{:S(2)}, u32[]{:S(2)}) %collective-permute-start) | collective-permute-done | bytes 2097184 | tf_op jit(solution)/shard_map/while/body/eval_jaxpr/ppermute | solution.py:16
  641.4 3.8 convert_divide_fusion.3
  645.3 2.7 constant_dynamic-slice_fusion.10
  661.6 6.3 fusion.117
  671.3 2.8 fusion.119
  674.1 17.4 %conditional.4 = (f32[2,768,4096]{1,2,0:T(8,128)}) conditional(s32[]{:T(128)} %convert_element_type.227, f32[2,768,4096]{1,2,0:T(8,128)} %get-tuple-element.430, (bf16[128,32,128]{2,0,1:T(8,128)(2,1)S(1)}, bf16[128,32,128]{0,2,1:T(8,128)(2,1)S(1)}, s32[]{:T(128)}, bf16[2,128,768]{2,1,0:T(8,128)(2,1)}, f32[2,768,4096]{1,2,0:T(8,128)}) %tuple.73), branch_computations={%region_6.6_spmd, %region_7.7_spmd} | conditional | flops 1617952768 | bytes 54722608 | solution.py:119
  674.7 16.7 %bitcast_add_fusion = f32[2,768,4096]{1,2,0:T(8,128)} fusion(f32[2,768,4096]{1,2,0:T(8,128)} %get-tuple-element.185, bf16[1,128,4096]{1,2,0:T(8,128)(2,1)S(1)} %bitcast.174, bf16[1,128,4096]{1,2,0:T(8,128)(2,1)S(1)} %bitcast.171, bf16[2,128,768]{2,1,0:T(8,128)(2,1)} %get-tuple-element.188, s32[]{:T(128)S(6)} %select_n.76), kind=kOutput, calls=%fused_computation | convolution fusion | flops 1617952768 | bytes 52625412 | tf_op jit(solution)/shard_map/while/body/eval_jaxpr/cond/branch_1_fun/rl,irc->ilc/dot_general | solution.py:115
  691.4 23.2 %collective-permute-done = bf16[128,8192]{0,1:T(8,128)(2,1)} collective-permute-done((bf16[128,8192]{0,1:T(8,128)(2,1)}, bf16[128,8192]{0,1:T(8,128)(2,1)}, u32[]{:S(2)}, u32[]{:S(2)}) %collective-permute-start) | collective-permute-done | bytes 2097184 | tf_op jit(solution)/shard_map/while/body/eval_jaxpr/ppermute | solution.py:16
  722.2 3.6 fusion.50
  727.7 2.8 multiply_convert_fusion.4
  731.3 21.0 %conditional.2 = (f32[2,768,4096]{1,2,0:T(8,128)}) conditional(s32[]{:T(128)} %convert_element_type.140, f32[2,768,4096]{1,2,0:T(8,128)} %get-tuple-element.218, (bf16[128,32,128]{2,0,1:T(8,128)(2,1)S(1)}, bf16[128,32,128]{0,2,1:T(8,128)(2,1)}, s32[]{:T(128)}, bf16[2,128,768]{2,1,0:T(8,128)(2,1)}, f32[2,768,4096]{1,2,0:T(8,128)}) %tuple.86), branch_computations={%region_14.15_spmd, %region_15.16_spmd} | conditional | flops 1617952768 | bytes 54722608 | solution.py:119
  732.0 20.3 %bitcast_add_fusion.1 = f32[2,768,4096]{1,2,0:T(8,128)} fusion(f32[2,768,4096]{1,2,0:T(8,128)} %get-tuple-element.205, bf16[1,128,4096]{1,2,0:T(8,128)(2,1)} %bitcast.188, bf16[1,128,4096]{1,2,0:T(8,128)(2,1)S(1)} %bitcast.183, bf16[2,128,768]{2,1,0:T(8,128)(2,1)} %get-tuple-element.208, s32[]{:T(128)S(6)} %select_n.85), kind=kOutput, calls=%fused_computation.53 | convolution fusion | flops 1617952768 | bytes 52625412 | tf_op jit(solution)/shard_map/cond/branch_1_fun/rl,irc->ilc/dot_general | solution.py:115
  752.3 13.1 %convert_element_type.146 = bf16[2,768,4096]{1,2,0:T(8,128)(2,1)} convert(f32[2,768,4096]{1,2,0:T(8,128)} %get-tuple-element.461) | non-fusion elementwise | flops 6291456 | bytes 37748736 | tf_op jit(solution)/shard_map/convert_element_type | solution.py:138
  767.4 3.0 copy.66
  770.5 3.2 copy.65
  773.6 129.5 %reduce-scatter.2.cloned.1.call-done = bf16[2,768,256]{1,2,0:T(8,128)(2,1)} async-done(((bf16[2,768,4096]{1,2,0:T(8,128)(2,1)}), bf16[2,768,256]{1,2,0:T(8,128)(2,1)}) %reduce-scatter.2.cloned.1.call-update) | async-done | bytes 786448 | tf_op jit(solution)/shard_map/reduce_scatter | solution.py:137
  903.1 4.7 fusion.63
  907.8 6.6 copy.52
  918.6 2.8 fusion.35
  921.4 4.9 fusion.40
  926.4 2.9 copy.64
  930.7 3.1 copy.72
  933.8 44.8 %all-gather.2.cloned.1.call-done = bf16[2,768,4096]{1,2,0:T(8,128)(2,1)} async-done(((bf16[2,768,256]{1,2,0:T(8,128)(2,1)}), bf16[2,768,4096]{1,2,0:T(8,128)(2,1)}) %all-gather.2.cloned.1.call-update) | async-done | bytes 12582928 | tf_op jit(solution)/shard_map/all_gather | solution.py:148
  978.6 8.0 fusion.34
  986.6 2.7 copy.73
  (266 shorter events, 230.4 us)
Async XLA Ops:
  7.2 971.4 %copy-start = (bf16[128,768]{1,0:T(8,128)(2,1)S(1)}, bf16[128,768]{1,0:T(8,128)(2,1)}, u32[]{:S(2)}) copy-start(bf16[128,768]{1,0:T(8,128)(2,1)} %param.21) | copy-start | bytes 589828
  7.2 895.9 %reduce-scatter.2.cloned.1.call-start = ((), (), s32[]{:S(2)}) async-start(), calls=%async_computation.1 | async-start | bytes 13369344 | tf_op jit(solution)/shard_map/reduce_scatter | solution.py:137
  11.8 7.2 copy-start.10
  21.5 2.7 copy-start.17
  24.2 2.7 copy-start.13
  24.8 3.2 copy-start.5
  59.6 2.9 copy-start.2
  59.6 4.0 copy-start.3
  65.8 2.6 copy-start.4
  82.2 49.8 %collective-permute-start = (bf16[128,8192]{0,1:T(8,128)(2,1)}, bf16[128,8192]{0,1:T(8,128)(2,1)}, u32[]{:S(2)}, u32[]{:S(2)}) collective-permute-start(bf16[128,8192]{0,1:T(8,128)(2,1)} %get-tuple-element.408), channel_id=1, source_target_pairs={{16,0},{32,16},{48,32},{64,48},{80,64},{96,80},{112,96},{17,1},{33... | collective-permute-start | bytes 6291464 | tf_op jit(solution)/shard_map/while/body/eval_jaxpr/ppermute | solution.py:16
  144.0 2.9 copy-start.2
  144.1 4.0 copy-start.3
  150.3 2.6 copy-start.4
  166.6 49.1 %collective-permute-start = (bf16[128,8192]{0,1:T(8,128)(2,1)}, bf16[128,8192]{0,1:T(8,128)(2,1)}, u32[]{:S(2)}, u32[]{:S(2)}) collective-permute-start(bf16[128,8192]{0,1:T(8,128)(2,1)} %get-tuple-element.408), channel_id=1, source_target_pairs={{16,0},{32,16},{48,32},{64,48},{80,64},{96,80},{112,96},{17,1},{33... | collective-permute-start | bytes 6291464 | tf_op jit(solution)/shard_map/while/body/eval_jaxpr/ppermute | solution.py:16
  227.7 2.9 copy-start.2
  227.8 4.0 copy-start.3
  234.0 2.6 copy-start.4
  250.3 48.2 %collective-permute-start = (bf16[128,8192]{0,1:T(8,128)(2,1)}, bf16[128,8192]{0,1:T(8,128)(2,1)}, u32[]{:S(2)}, u32[]{:S(2)}) collective-permute-start(bf16[128,8192]{0,1:T(8,128)(2,1)} %get-tuple-element.408), channel_id=1, source_target_pairs={{16,0},{32,16},{48,32},{64,48},{80,64},{96,80},{112,96},{17,1},{33... | collective-permute-start | bytes 6291464 | tf_op jit(solution)/shard_map/while/body/eval_jaxpr/ppermute | solution.py:16
  310.4 2.9 copy-start.2
  310.5 4.0 copy-start.3
  316.7 2.6 copy-start.4
  333.1 50.6 %collective-permute-start = (bf16[128,8192]{0,1:T(8,128)(2,1)}, bf16[128,8192]{0,1:T(8,128)(2,1)}, u32[]{:S(2)}, u32[]{:S(2)}) collective-permute-start(bf16[128,8192]{0,1:T(8,128)(2,1)} %get-tuple-element.408), channel_id=1, source_target_pairs={{16,0},{32,16},{48,32},{64,48},{80,64},{96,80},{112,96},{17,1},{33... | collective-permute-start | bytes 6291464 | tf_op jit(solution)/shard_map/while/body/eval_jaxpr/ppermute | solution.py:16
  395.6 2.9 copy-start.2
  395.7 4.0 copy-start.3
  401.9 2.6 copy-start.4
  418.3 49.5 %collective-permute-start = (bf16[128,8192]{0,1:T(8,128)(2,1)}, bf16[128,8192]{0,1:T(8,128)(2,1)}, u32[]{:S(2)}, u32[]{:S(2)}) collective-permute-start(bf16[128,8192]{0,1:T(8,128)(2,1)} %get-tuple-element.408), channel_id=1, source_target_pairs={{16,0},{32,16},{48,32},{64,48},{80,64},{96,80},{112,96},{17,1},{33... | collective-permute-start | bytes 6291464 | tf_op jit(solution)/shard_map/while/body/eval_jaxpr/ppermute | solution.py:16
  479.7 2.9 copy-start.2
  479.8 4.0 copy-start.3
  486.0 2.6 copy-start.4
  502.4 48.6 %collective-permute-start = (bf16[128,8192]{0,1:T(8,128)(2,1)}, bf16[128,8192]{0,1:T(8,128)(2,1)}, u32[]{:S(2)}, u32[]{:S(2)}) collective-permute-start(bf16[128,8192]{0,1:T(8,128)(2,1)} %get-tuple-element.408), channel_id=1, source_target_pairs={{16,0},{32,16},{48,32},{64,48},{80,64},{96,80},{112,96},{17,1},{33... | collective-permute-start | bytes 6291464 | tf_op jit(solution)/shard_map/while/body/eval_jaxpr/ppermute | solution.py:16
  563.0 2.9 copy-start.2
  563.0 4.0 copy-start.3
  569.2 2.6 copy-start.4
  585.6 47.7 %collective-permute-start = (bf16[128,8192]{0,1:T(8,128)(2,1)}, bf16[128,8192]{0,1:T(8,128)(2,1)}, u32[]{:S(2)}, u32[]{:S(2)}) collective-permute-start(bf16[128,8192]{0,1:T(8,128)(2,1)} %get-tuple-element.408), channel_id=1, source_target_pairs={{16,0},{32,16},{48,32},{64,48},{80,64},{96,80},{112,96},{17,1},{33... | collective-permute-start | bytes 6291464 | tf_op jit(solution)/shard_map/while/body/eval_jaxpr/ppermute | solution.py:16
  645.2 2.9 copy-start.2
  645.3 4.0 copy-start.3
  651.5 2.6 copy-start.4
  667.9 46.7 %collective-permute-start = (bf16[128,8192]{0,1:T(8,128)(2,1)}, bf16[128,8192]{0,1:T(8,128)(2,1)}, u32[]{:S(2)}, u32[]{:S(2)}) collective-permute-start(bf16[128,8192]{0,1:T(8,128)(2,1)} %get-tuple-element.408), channel_id=1, source_target_pairs={{16,0},{32,16},{48,32},{64,48},{80,64},{96,80},{112,96},{17,1},{33... | collective-permute-start | bytes 6291464 | tf_op jit(solution)/shard_map/while/body/eval_jaxpr/ppermute | solution.py:16
  714.6 4.0 copy-start.16
  717.1 1.3 copy-start.6
  718.4 0.6 copy-start.15
  718.4 1.2 copy-start.7
  718.4 1.5 copy-start.8
  722.1 3.6 copy-start.11
  722.1 3.6 copy-start.12
  765.5 213.1 %all-gather.2.cloned.1.call-start = ((), (), s32[]{:S(2)}) async-start(), calls=%async_computation.2 | async-start | bytes 13369344 | tf_op jit(solution)/shard_map/all_gather | solution.py:148
  907.8 6.6 copy-start.9
  916.6 1.9 copy-start.14
  918.6 2.9 copy-start.1
Sparse Core Ops, SparseCore 0:
  765.6 137.4 reduce-scatter.1
  907.9 70.6 all-gather.1
where the time goes:
time: 1000 us; the launch traced here: 996 us
  waiting for transfers between devices  498 us (50%)
  other arithmetic  175 us (18%)
  matrix products  151 us (15%)
  local copies, waits for them, and re-layouts  141 us (14%)
  between operations  14.9 us (1%)
  starting transfers between devices  10.3 us (1%)
    ppermute x8, waiting for transfers between devices, shifted(): lax.ppermute(value, axis, [(source, source + steps) for source in range(f...  324 us
    reduce_scatter x1, waiting for transfers between devices, body(): lax.psum_scatter(carry[2].astype(jnp.bfloat16), 'dp', scatter_dimension=2...  129 us
    dynamic_slice x27, local copies, waits for them, and re-layouts, pick_slot(): return lax.dynamic_index_in_dim(array, slot, 0, keepdims=False)  61.1 us
    select_n x8, other arithmetic, advance(): jnp.where(valid, lax.dynamic_update_index_in_dim(grad_buffer, grad_x, slo...  50.7 us
    all_gather x1, waiting for transfers between devices, body(): lax.all_gather(weights_low, 'dp', axis=2, tiled=True)  44.8 us
    dot_general x2, matrix products, add_term(): jnp.einsum('rl,irc->ilc', pick_slot(latents, slot), paired, preferred_ele...  37 us
    div x9, other arithmetic, attend_back(): normed = floats / root_mean  32.6 us
    unnamed x38, local copies, waits for them, and re-layouts  29.5 us
  transfers between devices with their start and end apart: 10, of which 10 were waited for; matrix products, arithmetic and copies ran while one was open for 9% of the time, Pallas kernels for 0%

commit v1 on v0

v1 whole, which is shorter than its diff:
```python
import functools
import math

import jax
import jax.numpy as jnp
from jax import lax
from jax.experimental import pallas as pl
from jax.experimental.pallas import tpu as pltpu
from jax.sharding import PartitionSpec as P

HEAD_DIM = 128
LATENTS = 64
CHUNK = 16
CHUNK2 = 32
NORM_ROWS = 16
ADAM_ROWS = 64
F32 = jnp.float32
BF16 = jnp.bfloat16
MESH = pl.DeviceIdType.MESH


def dot_nt(a, b):
    return lax.dot_general(a, b, (((1,), (1,)), ((), ())), preferred_element_type=F32)


def dot_tn(a, b):
    return lax.dot_general(a, b, (((0,), (0,)), ((), ())), preferred_element_type=F32)


def dot_nn(a, b):
    return jnp.dot(a, b, preferred_element_type=F32)


def kernel(
    n_sec, n_dp,
    hid_hbm, key_hbm, val_hbm, lat_hbm, nl_hbm, media_ref, cot_hbm, gate_ref, w_hbm, mf_hbm, ms_hbm,
    ig_hbm, nw_hbm, kv_hbm,
    hid, keys, vals, lat, inc, inc2, q, p, go, gs, gbuf, rinv, coef, maskf,
    lt_all, nl_all, snd, rcv, wts, mf, ms, grads, wlow, kvs,
    in_sem, out_sem, r1_send, r1_recv, r2_send, r2_recv,
    gat_send, gat_recv, a2a_send, a2a_recv, kv_send, kv_recv, loc_sem,
):
    sec, me = lax.axis_index("section"), lax.axis_index("dp")
    micro, block, width = hid_hbm.shape
    span = key_hbm.shape[2]
    rows_m = key_hbm.shape[1]
    lat_w = lat_hbm.shape[2]
    cols_d = w_hbm.shape[2]
    heads = span // HEAD_DIM
    heads_d = cols_d // HEAD_DIM
    tokens = micro * block
    n_chunks = tokens // CHUNK
    per_micro = n_chunks // micro
    n_chunks2 = tokens // CHUNK2
    n_y = n_dp // 4
    scale = 1.0 / math.sqrt(HEAD_DIM)
    core = lax.rem(me, 2)
    x_lo = lax.rem(me // 2, 2)
    y_at = me // 4
    top = sec == n_sec - 1
    early = sec < n_sec // 2

    def dp_dev(j):
        return (sec, j)

    barrier = pltpu.get_barrier_semaphore()

    @pl.loop(1, n_dp)
    def _(k):
        pl.semaphore_signal(barrier, inc=1, device_id=dp_dev(lax.rem(me + k, n_dp)), device_id_type=MESH)

    @pl.when(sec > 0)
    def _():
        pl.semaphore_signal(barrier, inc=1, device_id=(sec - 1, me), device_id_type=MESH)

    @pl.when(sec < n_sec - 1)
    def _():
        pl.semaphore_signal(barrier, inc=1, device_id=(sec + 1, me), device_id_type=MESH)

    def load(i, src, dst):
        return pltpu.make_async_copy(src, dst, in_sem.at[i])

    hid_loads = [load(m, hid_hbm.at[m], hid.at[pl.ds(m * block, block), :]) for m in range(micro)]
    key_loads = [load(2 + m, key_hbm.at[m], keys.at[m]) for m in range(micro)]
    val_loads = [load(4 + m, val_hbm.at[m], vals.at[m]) for m in range(micro)]
    lat_load = load(6, lat_hbm, lat)
    nl_load = load(7, nl_hbm, nl_all.at[pl.ds(me * block, block), :])
    w_load, mf_load, ms_load = load(8, w_hbm, wts), load(9, mf_hbm, mf), load(10, ms_hbm, ms)
    cot_loads = [load(11 + m, cot_hbm.at[m, :, pl.ds(0, span)], inc.at[pl.ds(m * block, block), :]) for m in range(micro)]
    cot2_loads = [
        load(13 + m, cot_hbm.at[m, :, pl.ds(span, width - span)], inc2.at[pl.ds(m * block, block), :])
        for m in range(micro)
    ]
    lat_load.start()
    nl_load.start()
    hid_loads[0].start()
    key_loads[0].start()

    @pl.when(top)
    def _():
        for c in cot_loads:
            c.start()

    val_loads[0].start()
    for c in (hid_loads[1], key_loads[1], val_loads[1], w_load, mf_load, ms_load):
        c.start()

    @pl.when(top)
    def _():
        for c in cot2_loads:
            c.start()

    for m in range(micro):
        row = media_ref[pl.ds(m, 1), :].astype(F32)
        maskf[m] = jnp.transpose(jnp.broadcast_to(row, (block, block)))
    lat_load.wait()
    nl_load.wait()
    my_rows = pl.ds(pl.multiple_of(me * rows_m, rows_m), rows_m)
    for m in range(micro):
        lt_all[m, :, my_rows] = jnp.transpose(lat[m].astype(F32)).astype(BF16)

    others = jnp.where(sec > 0, 1, 0) + jnp.where(sec < n_sec - 1, 1, 0) + n_dp - 1
    pl.semaphore_wait(barrier, others)

    def gather_copy(slot, owner, target):
        at = pl.ds(pl.multiple_of(owner * rows_m, rows_m), rows_m)
        ref_l = lt_all.at[:, :, at]
        ref_n = nl_all.at[at, :]
        return [
            pltpu.make_async_remote_copy(
                src_ref=ref, dst_ref=ref, send_sem=gat_send.at[i, slot], recv_sem=gat_recv.at[i, owner],
                device_id=dp_dev(target), device_id_type=MESH,
            )
            for i, ref in enumerate((ref_l, ref_n))
        ]

    def gather_start(slot, owner, target):
        for c in gather_copy(slot, owner, target):
            c.start()

    def gather_wait_recv(owner):
        for c in gather_copy(0, owner, me):
            c.wait_recv()

    def gather_wait_send(slot):
        for c in gather_copy(slot, me, me):
            c.wait_send()

    x_peer = me + 2 - 4 * x_lo
    core_peer = me + 1 - 2 * core

    def y_peer(dy):
        return lax.rem(y_at + dy, n_y) * 4 + x_lo * 2 + core

    gather_start(0, me, x_peer)
    for dy in range(1, n_y):
        gather_start(dy, me, y_peer(dy))

    def gather_second():
        gather_wait_recv(x_peer)
        for dy in range(1, n_y):
            gather_start(n_y - 1 + dy, x_peer, y_peer(dy))

    def gather_third():
        for dy in range(1, n_y):
            gather_wait_recv(y_peer(dy))
            gather_wait_recv(y_peer(dy) + 2 - 4 * x_lo)

        @pl.loop(0, n_dp // 2)
        def _(k):
            gather_start(2 * n_y - 1 + k, 2 * k + core, core_peer)

    def prepare(m):
        base = m * block

        @pl.loop(0, block // NORM_ROWS)
        def _(t):
            rows = pl.ds(pl.multiple_of(base + t * NORM_ROWS, NORM_ROWS), NORM_ROWS)
            total = jnp.zeros((NORM_ROWS, 128), F32)
            for c in range(width // 128):
                h = hid[rows, pl.ds(c * 128, 128)].astype(F32)
                total = total + h * h
            mean = jnp.sum(total, axis=1, keepdims=True) * (1.0 / width)
            r = jnp.broadcast_to(1.0 / jnp.sqrt(mean + 1e-06), (NORM_ROWS, 128))
            rinv[rows, :] = r
            for c in range(heads):
                cols = pl.ds(c * 128, 128)
                q[rows, cols] = (hid[rows, cols].astype(F32) * r).astype(BF16)

        rows = pl.ds(pl.multiple_of(base, block), block)
        half = lax.broadcasted_iota(jnp.int32, (block, rows_m), 1) // LATENTS
        allowed = half.astype(F32) == maskf[m]
        group = 4

        @pl.loop(0, heads // group)
        def _(hg):
            for j in range(group):
                cols = pl.ds(pl.multiple_of((hg * group + j) * 128, 128), 128)
                s = dot_nt(q[rows, cols], keys[m, :, cols]) * scale
                s = jnp.where(allowed, s, -1e30)
                e = jnp.exp(s - jnp.max(s, axis=1, keepdims=True))
                p[rows, cols] = e / jnp.sum(e, axis=1, keepdims=True)

    def relay1(c):
        rows = pl.ds(pl.multiple_of(c * CHUNK, CHUNK), CHUNK)
        return pltpu.make_async_remote_copy(
            src_ref=inc.at[rows, :], dst_ref=inc.at[rows, :], send_sem=r1_send.at[c], recv_sem=r1_recv.at[c],
            device_id=(jnp.maximum(sec - 1, 0), me), device_id_type=MESH,
        )

    def relay2(c):
        rows = pl.ds(pl.multiple_of(c * CHUNK2, CHUNK2), CHUNK2)
        return pltpu.make_async_remote_copy(
            src_ref=inc2.at[rows, :], dst_ref=inc2.at[rows, :], send_sem=r2_send.at[c], recv_sem=r2_recv.at[c],
            device_id=(jnp.maximum(sec - 1, 0), me), device_id_type=MESH,
        )

    gate_tanh = jnp.tanh(jnp.broadcast_to(gate_ref[...], (CHUNK, 128)))

    def chain_step(c):
        m = c // per_micro
        rows = pl.ds(pl.multiple_of(c * CHUNK, CHUNK), CHUNK)
        acc = jnp.zeros((CHUNK, 128), F32)
        for h in range(heads):
            cols = pl.ds(h * 128, 128)
            g = (gate_tanh * inc[rows, cols].astype(F32)).astype(BF16)
            go[rows, cols] = g
            gp = dot_nt(g, vals[m, :, cols])
            pr = p[rows, cols]
            weighted = jnp.sum(pr * gp, axis=1, keepdims=True)
            gsc = (pr * (gp - weighted)).astype(BF16)
            gs[rows, cols] = gsc
            gk = dot_nn(gsc, keys[m, :, cols])
            gbuf[:, cols] = gk
            acc = acc + gk * hid[rows, cols].astype(F32)
        r = rinv[rows, :]
        dots = jnp.sum(acc, axis=1, keepdims=True)
        a = r * scale
        b = r * r * r * (dots * (scale / width))
        coef[rows, :] = b
        for h in range(heads):
            cols = pl.ds(h * 128, 128)
            new = inc[rows, cols].astype(F32) + (a * gbuf[:, cols] - b * hid[rows, cols].astype(F32))
            inc[rows, cols] = new.astype(BF16)

    def second_step(c):
        @pl.when(jnp.logical_not(top))
        def _():
            relay2(c).wait_recv()

        for t in range(CHUNK2 // 16):
            rows = pl.ds(pl.multiple_of(c * CHUNK2 + t * 16, 16), 16)
            b = coef[rows, :]
            for h in range((width - span) // 128):
                cols, hcols = pl.ds(h * 128, 128), pl.ds(span + h * 128, 128)
                inc2[rows, cols] = (inc2[rows, cols].astype(F32) - b * hid[rows, hcols].astype(F32)).astype(BF16)

        @pl.when(sec > 0)
        def _():
            relay2(c).start()

    def a2a_copy(m, j, target):
        return pltpu.make_async_remote_copy(
            src_ref=snd.at[m, j], dst_ref=rcv.at[m, my_rows, :], send_sem=a2a_send.at[m, j],
            recv_sem=a2a_recv.at[m, me], device_id=dp_dev(target), device_id_type=MESH,
        )

    def a2a_own(m):
        return pltpu.make_async_copy(snd.at[m, me], rcv.at[m, my_rows, :], loc_sem.at[m])

    def project(m, k):
        j = lax.rem(me + k, n_dp)
        rows = pl.ds(pl.multiple_of(m * block, block), block)
        for i in range(heads_d):
            cols = pl.ds(pl.multiple_of(j * cols_d + i * 128, 128), 128)
            gk = dot_tn(gs[rows, cols], q[rows, cols]) * scale
            gv = dot_tn(p[rows, cols].astype(BF16), go[rows, cols])
            snd[m, j, :, pl.ds(i * 128, 128)] = gk.astype(BF16)
            snd[m, j, :, pl.ds(cols_d + i * 128, 128)] = gv.astype(BF16)

        @pl.when(k > 0)
        def _():
            a2a_copy(m, j, j).start()

        @pl.when(k == 0)
        def _():
            a2a_own(m).start()

    def a2a_wait(m):
        a2a_own(m).wait()

        @pl.loop(1, n_dp)
        def _(k):
            j = lax.rem(me + k, n_dp)
            at = pl.ds(pl.multiple_of(j * rows_m, rows_m), rows_m)
            pltpu.make_async_remote_copy(
                src_ref=snd.at[m, j], dst_ref=rcv.at[m, at, :], send_sem=a2a_send.at[m, j],
                recv_sem=a2a_recv.at[m, j], device_id=dp_dev(j), device_id_type=MESH,
            ).wait_recv()

    def weight_grad(m):
        tile = 128

        @pl.loop(0, lat_w // tile)
        def _(t):
            at = pl.ds(pl.multiple_of(t * tile, tile), tile)
            part = dot_nn(lt_all[m, at, :], rcv[m])
            if m == 0:
                grads[at, :] = part
            else:
                grads[at, :] += part

    for c in (hid_loads[0], key_loads[0]):
        c.wait()
    prepare(0)
    for c in (hid_loads[1], key_loads[1], val_loads[0], val_loads[1]):
        c.wait()

    @pl.when(jnp.logical_not(top))
    def _():
        prepare(1)

    @pl.when(top)
    def _():
        for c in cot_loads:
            c.wait()

    @pl.when(early)
    def _():
        gather_second()

    @pl.loop(0, n_chunks)
    def _(c):
        @pl.when(jnp.logical_and(c == per_micro, top))
        def _():
            prepare(1)

        @pl.when(jnp.logical_and(c == per_micro, jnp.logical_not(early)))
        def _():
            gather_second()

        @pl.when(jnp.logical_and(c == per_micro + per_micro // 2, early))
        def _():
            gather_third()

        @pl.when(jnp.logical_not(top))
        def _():
            relay1(c).wait_recv()

        chain_step(c)

        @pl.when(sec > 0)
        def _():
            relay1(c).start()

        share = n_dp // per_micro

        @pl.when(c >= per_micro)
        def _():
            for i in range(share):
                project(0, (c - per_micro) * share + i)

    out_first = [
        pltpu.make_async_copy(inc.at[pl.ds(m * block, block), :], ig_hbm.at[m, :, pl.ds(0, span)], out_sem.at[m])
        for m in range(micro)
    ]
    for c in out_first:
        c.start()

    @pl.loop(0, n_dp)
    def _(k):
        project(1, k)

    @pl.when(jnp.logical_not(early))
    def _():
        gather_third()

    @pl.when(top)
    def _():
        for c in cot2_loads:
            c.wait()

    @pl.loop(0, n_chunks2 // 2)
    def _(c):
        second_step(c)

    @pl.loop(0, n_dp // 2)
    def _(k):
        gather_wait_recv(2 * k + 1 - core)

    a2a_wait(0)
    weight_grad(0)
    for c in (w_load, mf_load, ms_load):
        c.wait()
    a2a_wait(1)
    weight_grad(1)

    @pl.loop(0, lat_w // ADAM_ROWS)
    def _(t):
        at = pl.ds(pl.multiple_of(t * ADAM_ROWS, ADAM_ROWS), ADAM_ROWS)
        for i in range(2):
            cols = pl.ds(i * cols_d, cols_d)
            g = grads[at, cols]
            cur = wts[i, at, :]
            first = 0.9 * mf[i, at, :] + 0.1 * g
            second = 0.95 * ms[i, at, :] + 0.05 * g * g
            new = cur - 0.02 * (first / (jnp.sqrt(second) + 1e-08) + 0.1 * cur)
            wts[i, at, :] = new
            wlow[at, cols] = new.astype(BF16)

    out_w = pltpu.make_async_copy(wts, nw_hbm, out_sem.at[2])
    out_w.start()

    my_cols = pl.ds(pl.multiple_of(me * cols_d, cols_d), cols_d)

    def kv_copy(j, source):
        cols = pl.ds(pl.multiple_of(source * cols_d, cols_d), cols_d)
        return pltpu.make_async_remote_copy(
            src_ref=kvs.at[j], dst_ref=kv_hbm.at[:, :, cols], send_sem=kv_send.at[j],
            recv_sem=kv_recv.at[source], device_id=dp_dev(j), device_id_type=MESH,
        )

    kv_own = pltpu.make_async_copy(kvs.at[me], kv_hbm.at[:, :, my_cols], loc_sem.at[2])

    @pl.loop(0, n_dp // 2)
    def _(k):
        pair = lax.rem(me // 2 + 1 + k, n_dp // 2)
        at = pl.ds(pl.multiple_of(pair * 2 * block, 2 * block), 2 * block)
        out = dot_nn(nl_all[at, :], wlow[...]).astype(BF16)
        for i in range(2):
            for kind in range(2):
                kvs[2 * pair + i, kind] = out[i * block : (i + 1) * block, kind * cols_d : (kind + 1) * cols_d]

        @pl.when(k < n_dp // 2 - 1)
        def _():
            for i in range(2):
                kv_copy(2 * pair + i, me).start()

        @pl.when(k == n_dp // 2 - 1)
        def _():
            kv_copy(core_peer, me).start()
            kv_own.start()

    @pl.loop(n_chunks2 // 2, n_chunks2)
    def _(c):
        second_step(c)

    out_second = [
        pltpu.make_async_copy(inc2.at[pl.ds(m * block, block), :], ig_hbm.at[m, :, pl.ds(span, width - span)], out_sem.at[3 + m])
        for m in range(micro)
    ]
    for c in out_second:
        c.start()

    @pl.when(sec > 0)
    def _():
        @pl.loop(0, n_chunks)
        def _(c):
            relay1(c).wait_send()

        @pl.loop(0, n_chunks2)
        def _(c):
            relay2(c).wait_send()

    @pl.loop(0, 2 * n_y - 1 + n_dp // 2)
    def _(k):
        gather_wait_send(k)

    for m in range(micro):
        @pl.loop(1, n_dp)
        def _(k):
            j = lax.rem(me + k, n_dp)
            a2a_copy(m, j, j).wait_send()

    @pl.loop(1, n_dp)
    def _(k):
        j = lax.rem(me + k, n_dp)
        kv_copy(j, me).wait_send()
        kv_copy(j, j).wait_recv()

    kv_own.wait()
    out_w.wait()
    for c in out_first + out_second:
        c.wait()


def body(
    hidden_states, key_rows, value_rows, latents, next_latents, media_index, cotangent, gate_alpha,
    weights, moment_first, moment_second,
):
    n_sec, n_dp = lax.axis_size("section"), lax.axis_size("dp")
    _, micro, block, width = hidden_states.shape
    span, rows_m = key_rows.shape[3], key_rows.shape[2]
    lat_w, cols_d = weights.shape[2], weights.shape[3]
    tokens = micro * block
    n_y = n_dp // 4
    n_chunks, n_chunks2 = tokens // CHUNK, tokens // CHUNK2
    any_spec = pl.BlockSpec(memory_space=pl.ANY)
    vmem_spec = pl.BlockSpec(memory_space=pltpu.VMEM)
    dma = pltpu.SemaphoreType.DMA
    vmem = pltpu.VMEM
    grad_in, new_w, kv = pl.pallas_call(
        functools.partial(kernel, n_sec, n_dp),
        out_shape=(
            jax.ShapeDtypeStruct((micro, block, width), BF16),
            jax.ShapeDtypeStruct((2, lat_w, cols_d), F32),
            jax.ShapeDtypeStruct((2, rows_m, span), BF16),
        ),
        in_specs=[any_spec] * 5 + [vmem_spec, any_spec, vmem_spec] + [any_spec] * 3,
        out_specs=(any_spec, any_spec, any_spec),
        scratch_shapes=[
            vmem((tokens, width), BF16),
            vmem((micro, rows_m, span), BF16),
            vmem((micro, rows_m, span), BF16),
            vmem((micro, rows_m, lat_w), BF16),
            vmem((tokens, span), BF16),
            vmem((tokens, width - span), BF16),
            vmem((tokens, span), BF16),
            vmem((tokens, span), F32),
            vmem((tokens, span), BF16),
            vmem((tokens, span), BF16),
            vmem((CHUNK, span), F32),
            vmem((tokens, 128), F32),
            vmem((tokens, 128), F32),
            vmem((micro, block, rows_m), F32),
            vmem((micro, lat_w, n_dp * rows_m), BF16),
            vmem((n_dp * block, lat_w), BF16),
            vmem((micro, n_dp, rows_m, 2 * cols_d), BF16),
            vmem((micro, n_dp * rows_m, 2 * cols_d), BF16),
            vmem((2, lat_w, cols_d), F32),
            vmem((2, lat_w, cols_d), F32),
            vmem((2, lat_w, cols_d), F32),
            vmem((lat_w, 2 * cols_d), F32),
            vmem((lat_w, 2 * cols_d), BF16),
            vmem((n_dp, 2, block, cols_d), BF16),
            dma((15,)),
            dma((5,)),
            dma((n_chunks,)),
            dma((n_chunks,)),
            dma((n_chunks2,)),
            dma((n_chunks2,)),
            dma((2, 2 * n_y - 1 + n_dp // 2)),
            dma((2, n_dp)),
            dma((micro, n_dp)),
            dma((micro, n_dp)),
            dma((n_dp,)),
            dma((n_dp,)),
            dma((3,)),
        ],
        compiler_params=pltpu.CompilerParams(
            collective_id=0, has_side_effects=True, vmem_limit_bytes=62 * 1024 * 1024
        ),
    )(
        hidden_states[0], key_rows[0], value_rows[0], latents, next_latents, media_index, cotangent,
        gate_alpha.reshape(1, 1), weights[0], moment_first[0], moment_second[0],
    )
    return grad_in[None], new_w[None], kv[None]


def solution(mesh):
    in_specs = (
        P("section", None, "dp", None),
        P("section", None, "dp", None),
        P("section", None, "dp", None),
        P(None, "dp", None),
        P("dp", None),
        P(None, "dp"),
        P(None, "dp", None),
        P("section"),
        P("section", None, None, "dp"),
        P("section", None, None, "dp"),
        P("section", None, None, "dp"),
    )
    out_specs = (
        P("section", None, "dp", None),
        P("section", None, None, "dp"),
        P("section", None, "dp", None),
    )
    return jax.shard_map(body, mesh=mesh, in_specs=in_specs, out_specs=out_specs, check_vma=False)
```

time: 1000 us -> 309 us (0.31)
  waiting for transfers between devices: 498 us -> 0 us
  Pallas kernels: 0 us -> 299 us
  other arithmetic: 175 us -> 0 us
  matrix products: 151 us -> 0 us
  local copies, waits for them, and re-layouts: 141 us -> 8.24 us
  between operations: 14.9 us -> 1.3 us
  starting transfers between devices: 10.3 us -> 0 us
    ppermute x8 -> x0, waiting for transfers between devices: 324 us -> none  [shifted(): lax.ppermute(value, axis, [(source, source + steps) for source in range(f...]
    pallas_call x0 -> x1, Pallas kernels: none -> 299 us  [body(): pl.pallas_call(functools.partial(kernel, n_sec, n_dp), out_shape=(jax.Sha...]
    dot_general x39 -> x0, matrix products: 131 us -> none  [the longest x2 37 us: add_term(): jnp.einsum('rl,irc->ilc', pick_slot(latents, slot), paired, preferred_ele...]
    reduce_scatter x1 -> x0, waiting for transfers between devices: 129 us -> none  [body(): lax.psum_scatter(carry[2].astype(jnp.bfloat16), 'dp', scatter_dimension=2...]
    dynamic_slice x35 -> x0, local copies, waits for them, and re-layouts: 65.8 us -> none  [the longest x27 61.1 us: pick_slot(): return lax.dynamic_index_in_dim(array, slot, 0, keepdims=False)]
    select_n x18 -> x0, other arithmetic: 53.7 us -> none  [the longest x8 50.7 us: advance(): jnp.where(valid, lax.dynamic_update_index_in_dim(grad_buffer, grad_x, slo...]
    reduce_sum x18 -> x0, other arithmetic: 48.6 us -> none  [the longest x9 24.4 us: attend_back(): inner = jnp.mean(grad_normed * normed, axis=1, keepdims=True)]
    all_gather x1 -> x0, waiting for transfers between devices: 44.8 us -> none  [body(): lax.all_gather(weights_low, 'dp', axis=2, tiled=True)]
  transfers between devices with their start and end apart: 10 -> 0, of which waited for: 10 -> 0; matrix products, arithmetic and copies ran while one was open for 9% -> 0% of each run, Pallas kernels for 0% -> 0%
where the time goes in v1:
time: 309 us
  Pallas kernels  299 us (97%)
  local copies, waits for them, and re-layouts  8.24 us (3%)
    pallas_call x1, Pallas kernels, body(): pl.pallas_call(functools.partial(kernel, n_sec, n_dp), out_shape=(jax.Sha...  299 us
    unnamed x7, local copies, waits for them, and re-layouts  8.24 us

profile of v1, /device:TPU:0, one launch (start us, length us, event | category | flops | bytes accessed | tf_op | source)
XLA Modules:
  0.0 308.6 jit_solution(7276733835928811468)
XLA Ops:
  1.3 299.0 %shard_map.130 = (bf16[2,128,8192]{2,1,0:T(8,128)(2,1)}, f32[2,768,256]{2,1,0:T(8,128)}, bf16[2,128,4096]{2,1,0:T(8,128)(2,1)}) custom-call(bf16[2,128,8192]{2,1,0:T(8,128)(2,1)} %bitcast.12, bf16[2,128,4096]{2,1,0:T(8,128)(2,1)} %bitcast.14, bf16[2,128,4096]{2,1,0:T(8,128)(2,1)} %bitcast.15, bf16[2,128,768]{2,1,0:T(8,128)(2,1)} %lat_hbm.1, ...), custom_call_target="tpu_custom_call" | custom-call | tf_op jit(solution)/shard_map/pallas_call | solution.py:502
  300.3 0.0 copy-start.1
  300.3 4.8 %copy.18 = bf16[1,2,128,8192]{3,2,1,0:T(8,128)(2,1)} copy(bf16[1,2,128,8192]{3,2,1,0:T(8,128)(2,1)} %bitcast.11) | data formatting | bytes 8388608
  305.1 0.0 copy-done.1
  305.1 0.0 copy-start
  305.1 1.1 copy.19
  306.2 1.0 copy-done
  307.2 1.3 copy.20
Async XLA Ops:
  300.3 4.8 %copy-start.1 = (f32[2,768,256]{2,1,0:T(8,128)S(1)}, f32[2,768,256]{2,1,0:T(8,128)}, u32[]{:S(2)}) copy-start(f32[2,768,256]{2,1,0:T(8,128)} %get-tuple-element.7) | copy-start | bytes 4718596
  305.1 2.2 copy-start

commit v2 on v1

--- a/solution.py
+++ b/solution.py
@@ -35,7 +35,7 @@
     n_sec, n_dp,
     hid_hbm, key_hbm, val_hbm, lat_hbm, nl_hbm, media_ref, cot_hbm, gate_ref, w_hbm, mf_hbm, ms_hbm,
     ig_hbm, nw_hbm, kv_hbm,
-    hid, keys, vals, lat, inc, inc2, q, p, go, gs, gbuf, rinv, coef, maskf,
+    hid, keys, vals, lat, inc, inc2, q, p, go, gs, gpbuf, gbuf, rinv, coef, maskf,
     lt_all, nl_all, snd, rcv, wts, mf, ms, grads, wlow, kvs,
     in_sem, out_sem, r1_send, r1_recv, r2_send, r2_recv,
     gat_send, gat_recv, a2a_send, a2a_recv, kv_send, kv_recv, loc_sem,
@@ -201,6 +201,13 @@
                 e = jnp.exp(s - jnp.max(s, axis=1, keepdims=True))
                 p[rows, cols] = e / jnp.sum(e, axis=1, keepdims=True)
 
+    def transpose_values(m):
+        @pl.loop(0, heads // 4)
+        def _(hg):
+            for j in range(4):
+                cols = pl.ds(pl.multiple_of((hg * 4 + j) * 128, 128), 128)
+                vals[m, :, cols] = jnp.transpose(vals[m, :, cols])
+
     def relay1(c):
         rows = pl.ds(pl.multiple_of(c * CHUNK, CHUNK), CHUNK)
         return pltpu.make_async_remote_copy(
@@ -220,17 +227,20 @@
     def chain_step(c):
         m = c // per_micro
         rows = pl.ds(pl.multiple_of(c * CHUNK, CHUNK), CHUNK)
-        acc = jnp.zeros((CHUNK, 128), F32)
         for h in range(heads):
             cols = pl.ds(h * 128, 128)
             g = (gate_tanh * inc[rows, cols].astype(F32)).astype(BF16)
             go[rows, cols] = g
-            gp = dot_nt(g, vals[m, :, cols])
-            pr = p[rows, cols]
+            gpbuf[:, cols] = dot_nn(g, vals[m, :, cols])
+        for h in range(heads):
+            cols = pl.ds(h * 128, 128)
+            pr, gp = p[rows, cols], gpbuf[:, cols]
             weighted = jnp.sum(pr * gp, axis=1, keepdims=True)
-            gsc = (pr * (gp - weighted)).astype(BF16)
-            gs[rows, cols] = gsc
-            gk = dot_nn(gsc, keys[m, :, cols])
+            gs[rows, cols] = (pr * (gp - weighted)).astype(BF16)
+        acc = jnp.zeros((CHUNK, 128), F32)
+        for h in range(heads):
+            cols = pl.ds(h * 128, 128)
+            gk = dot_nn(gs[rows, cols], keys[m, :, cols])
             gbuf[:, cols] = gk
             acc = acc + gk * hid[rows, cols].astype(F32)
         r = rinv[rows, :]
@@ -270,6 +280,17 @@
 
     def project(m, k):
         j = lax.rem(me + k, n_dp)
+        project_compute(m, j)
+
+        @pl.when(k > 0)
+        def _():
+            a2a_copy(m, j, j).start()
+
+        @pl.when(k == 0)
+        def _():
+            a2a_own(m).start()
+
+    def project_compute(m, j):
         rows = pl.ds(pl.multiple_of(m * block, block), block)
         for i in range(heads_d):
             cols = pl.ds(pl.multiple_of(j * cols_d + i * 128, 128), 128)
@@ -277,14 +298,6 @@
             gv = dot_tn(p[rows, cols].astype(BF16), go[rows, cols])
             snd[m, j, :, pl.ds(i * 128, 128)] = gk.astype(BF16)
             snd[m, j, :, pl.ds(cols_d + i * 128, 128)] = gv.astype(BF16)
-
-        @pl.when(k > 0)
-        def _():
-            a2a_copy(m, j, j).start()
-
-        @pl.when(k == 0)
-        def _():
-            a2a_own(m).start()
 
     def a2a_wait(m):
         a2a_own(m).wait()
@@ -313,12 +326,15 @@
     for c in (hid_loads[0], key_loads[0]):
         c.wait()
     prepare(0)
-    for c in (hid_loads[1], key_loads[1], val_loads[0], val_loads[1]):
+    val_loads[0].wait()
+    transpose_values(0)
+    for c in (hid_loads[1], key_loads[1], val_loads[1]):
         c.wait()
 
     @pl.when(jnp.logical_not(top))
     def _():
         prepare(1)
+        transpose_values(1)
 
     @pl.when(top)
     def _():
@@ -334,6 +350,7 @@
         @pl.when(jnp.logical_and(c == per_micro, top))
         def _():
             prepare(1)
+            transpose_values(1)
 
         @pl.when(jnp.logical_and(c == per_micro, jnp.logical_not(early)))
         def _():
@@ -520,6 +537,7 @@
             vmem((tokens, span), BF16),
             vmem((tokens, span), BF16),
             vmem((CHUNK, span), F32),
+            vmem((CHUNK, span), F32),
             vmem((tokens, 128), F32),
             vmem((tokens, 128), F32),
             vmem((micro, block, rows_m), F32),

time: 309 us -> 228 us (0.74)
  Pallas kernels: 299 us -> 218 us
    pallas_call x1, Pallas kernels: 299 us -> 218 us  [body(): pl.pallas_call(functools.partial(kernel, n_sec, n_dp), out_shape=(jax.Sha...]
where the time goes in v2:
time: 228 us
  Pallas kernels  218 us (96%)
  local copies, waits for them, and re-layouts  8.24 us (4%)
    pallas_call x1, Pallas kernels, body(): pl.pallas_call(functools.partial(kernel, n_sec, n_dp), out_shape=(jax.Sha...  218 us
    unnamed x7, local copies, waits for them, and re-layouts  8.24 us

profile of v2, /device:TPU:0, one launch (start us, length us, event | category | flops | bytes accessed | tf_op | source)
XLA Modules:
  0.0 228.0 jit_solution(16489390117387268404)
XLA Ops:
  1.3 218.5 %shard_map.130 = (bf16[2,128,8192]{2,1,0:T(8,128)(2,1)}, f32[2,768,256]{2,1,0:T(8,128)}, bf16[2,128,4096]{2,1,0:T(8,128)(2,1)}) custom-call(bf16[2,128,8192]{2,1,0:T(8,128)(2,1)} %bitcast.12, bf16[2,128,4096]{2,1,0:T(8,128)(2,1)} %bitcast.14, bf16[2,128,4096]{2,1,0:T(8,128)(2,1)} %bitcast.15, bf16[2,128,768]{2,1,0:T(8,128)(2,1)} %lat_hbm.1, ...), custom_call_target="tpu_custom_call" | custom-call | tf_op jit(solution)/shard_map/pallas_call | solution.py:519
  219.8 0.0 copy-start.1
  219.8 4.8 %copy.18 = bf16[1,2,128,8192]{3,2,1,0:T(8,128)(2,1)} copy(bf16[1,2,128,8192]{3,2,1,0:T(8,128)(2,1)} %bitcast.11) | data formatting | bytes 8388608
  224.5 0.0 copy-done.1
  224.5 0.0 copy-start
  224.5 1.1 copy.19
  225.7 1.0 copy-done
  226.7 1.3 copy.20
Async XLA Ops:
  219.8 4.8 %copy-start.1 = (f32[2,768,256]{2,1,0:T(8,128)S(1)}, f32[2,768,256]{2,1,0:T(8,128)}, u32[]{:S(2)}) copy-start(f32[2,768,256]{2,1,0:T(8,128)} %get-tuple-element.7) | copy-start | bytes 4718596
  224.5 2.2 copy-start

commit v3 on v2

--- a/solution.py
+++ b/solution.py
@@ -11,9 +11,13 @@
 HEAD_DIM = 128
 LATENTS = 64
 CHUNK = 16
-CHUNK2 = 32
+CHUNK2 = 16
 NORM_ROWS = 16
+TOP_ROWS = 32
+OWNERS = 4
+GROUP = 8
 ADAM_ROWS = 64
+WG_ROWS = 256
 F32 = jnp.float32
 BF16 = jnp.bfloat16
 MESH = pl.DeviceIdType.MESH
@@ -35,10 +39,10 @@
     n_sec, n_dp,
     hid_hbm, key_hbm, val_hbm, lat_hbm, nl_hbm, media_ref, cot_hbm, gate_ref, w_hbm, mf_hbm, ms_hbm,
     ig_hbm, nw_hbm, kv_hbm,
-    hid, keys, vals, lat, inc, inc2, q, p, go, gs, gpbuf, gbuf, rinv, coef, maskf,
-    lt_all, nl_all, snd, rcv, wts, mf, ms, grads, wlow, kvs,
+    hid, keys, vals, lat, inc, inc2, q, p, go, gs, sbuf, gpbuf, gbuf, rinv, coef, maskf,
+    lt_all, nl_all, snd, rcv, wts, mf, ms, grads, wlow, kvs, fwd,
     in_sem, out_sem, r1_send, r1_recv, r2_send, r2_recv,
-    gat_send, gat_recv, a2a_send, a2a_recv, kv_send, kv_recv, loc_sem,
+    f_send, gat_send, gat_recv, a2a_send, a2a_recv, kv_send, kv_recv, loc_sem,
 ):
     sec, me = lax.axis_index("section"), lax.axis_index("dp")
     micro, block, width = hid_hbm.shape
@@ -58,7 +62,10 @@
     x_lo = lax.rem(me // 2, 2)
     y_at = me // 4
     top = sec == n_sec - 1
-    early = sec < n_sec // 2
+    mid_at = n_sec // 2
+    early = sec < mid_at
+    detour = mid_at < n_sec - 1
+    mid = jnp.logical_and(sec == mid_at, detour)
 
     def dp_dev(j):
         return (sec, j)
@@ -76,6 +83,20 @@
     @pl.when(sec < n_sec - 1)
     def _():
         pl.semaphore_signal(barrier, inc=1, device_id=(sec + 1, me), device_id_type=MESH)
+
+    def ring_pairs(do):
+        if detour:
+            for one, two in ((mid_at, n_sec - 1), (n_sec - 1, mid_at - 1)):
+                if one - two != 1 and two - one != 1:
+                    for a, b in ((one, two), (two, one)):
+                        do(a, b)
+
+    def greet(a, b):
+        @pl.when(sec == a)
+        def _():
+            pl.semaphore_signal(barrier, inc=1, device_id=(b, me), device_id_type=MESH)
+
+    ring_pairs(greet)
 
     def load(i, src, dst):
         return pltpu.make_async_copy(src, dst, in_sem.at[i])
@@ -120,7 +141,13 @@
         lt_all[m, :, my_rows] = jnp.transpose(lat[m].astype(F32)).astype(BF16)
 
     others = jnp.where(sec > 0, 1, 0) + jnp.where(sec < n_sec - 1, 1, 0) + n_dp - 1
-    pl.semaphore_wait(barrier, others)
+    extra = [others]
+
+    def expect(a, b):
+        extra[0] = extra[0] + jnp.where(sec == a, 1, 0)
+
+    ring_pairs(expect)
+    pl.semaphore_wait(barrier, extra[0])
 
     def gather_copy(slot, owner, target):
         at = pl.ds(pl.multiple_of(owner * rows_m, rows_m), rows_m)
@@ -170,12 +197,10 @@
         def _(k):
             gather_start(2 * n_y - 1 + k, 2 * k + core, core_peer)
 
-    def prepare(m):
-        base = m * block
-
-        @pl.loop(0, block // NORM_ROWS)
+    def prepare(m, start, count):
+        @pl.loop(0, count // NORM_ROWS)
         def _(t):
-            rows = pl.ds(pl.multiple_of(base + t * NORM_ROWS, NORM_ROWS), NORM_ROWS)
+            rows = pl.ds(pl.multiple_of(m * block + start + t * NORM_ROWS, NORM_ROWS), NORM_ROWS)
             total = jnp.zeros((NORM_ROWS, 128), F32)
             for c in range(width // 128):
                 h = hid[rows, pl.ds(c * 128, 128)].astype(F32)
@@ -187,17 +212,18 @@
                 cols = pl.ds(c * 128, 128)
                 q[rows, cols] = (hid[rows, cols].astype(F32) * r).astype(BF16)
 
-        rows = pl.ds(pl.multiple_of(base, block), block)
-        half = lax.broadcasted_iota(jnp.int32, (block, rows_m), 1) // LATENTS
-        allowed = half.astype(F32) == maskf[m]
-        group = 4
-
-        @pl.loop(0, heads // group)
+        rows = pl.ds(pl.multiple_of(m * block + start, count), count)
+        half = lax.broadcasted_iota(jnp.int32, (count, rows_m), 1) // LATENTS
+        allowed = half.astype(F32) == maskf[m, pl.ds(pl.multiple_of(start, count), count), :]
+
+        @pl.loop(0, heads // GROUP)
         def _(hg):
-            for j in range(group):
-                cols = pl.ds(pl.multiple_of((hg * group + j) * 128, 128), 128)
-                s = dot_nt(q[rows, cols], keys[m, :, cols]) * scale
-                s = jnp.where(allowed, s, -1e30)
+            for j in range(GROUP):
+                cols = pl.ds(pl.multiple_of((hg * GROUP + j) * 128, 128), 128)
+                sbuf[pl.ds(0, count), pl.ds(j * 128, 128)] = dot_nt(q[rows, cols], keys[m, :, cols])
+            for j in range(GROUP):
+                cols = pl.ds(pl.multiple_of((hg * GROUP + j) * 128, 128), 128)
+                s = jnp.where(allowed, sbuf[pl.ds(0, count), pl.ds(j * 128, 128)] * scale, -1e30)
                 e = jnp.exp(s - jnp.max(s, axis=1, keepdims=True))
                 p[rows, cols] = e / jnp.sum(e, axis=1, keepdims=True)
 
@@ -215,23 +241,30 @@
             device_id=(jnp.maximum(sec - 1, 0), me), device_id_type=MESH,
         )
 
-    def relay2(c):
+    def relay2(c, dst=inc2, to=None):
         rows = pl.ds(pl.multiple_of(c * CHUNK2, CHUNK2), CHUNK2)
         return pltpu.make_async_remote_copy(
-            src_ref=inc2.at[rows, :], dst_ref=inc2.at[rows, :], send_sem=r2_send.at[c], recv_sem=r2_recv.at[c],
-            device_id=(jnp.maximum(sec - 1, 0), me), device_id_type=MESH,
+            src_ref=inc2.at[rows, :], dst_ref=dst.at[rows, :], send_sem=r2_send.at[c], recv_sem=r2_recv.at[c],
+            device_id=(jnp.maximum(sec - 1, 0) if to is None else to, me), device_id_type=MESH,
         )
 
+    def forward2(c):
+        rows = pl.ds(pl.multiple_of(c * CHUNK2, CHUNK2), CHUNK2)
+        return pltpu.make_async_remote_copy(
+            src_ref=fwd.at[rows, :], dst_ref=inc2.at[rows, :], send_sem=f_send.at[c], recv_sem=r2_recv.at[c],
+            device_id=(mid_at - 1, me), device_id_type=MESH,
+        )
+
     gate_tanh = jnp.tanh(jnp.broadcast_to(gate_ref[...], (CHUNK, 128)))
 
-    def chain_step(c):
+    def chain_step(c, dot_values):
         m = c // per_micro
         rows = pl.ds(pl.multiple_of(c * CHUNK, CHUNK), CHUNK)
         for h in range(heads):
             cols = pl.ds(h * 128, 128)
             g = (gate_tanh * inc[rows, cols].astype(F32)).astype(BF16)
             go[rows, cols] = g
-            gpbuf[:, cols] = dot_nn(g, vals[m, :, cols])
+            gpbuf[:, cols] = dot_values(g, vals[m, :, cols])
         for h in range(heads):
             cols = pl.ds(h * 128, 128)
             pr, gp = p[rows, cols], gpbuf[:, cols]
@@ -265,93 +298,165 @@
                 cols, hcols = pl.ds(h * 128, 128), pl.ds(span + h * 128, 128)
                 inc2[rows, cols] = (inc2[rows, cols].astype(F32) - b * hid[rows, hcols].astype(F32)).astype(BF16)
 
-        @pl.when(sec > 0)
+        @pl.when(jnp.logical_and(sec > 0, jnp.logical_not(mid)))
         def _():
             relay2(c).start()
 
-    def a2a_copy(m, j, target):
+        if detour:
+            @pl.when(mid)
+            def _():
+                relay2(c, fwd, n_sec - 1).start()
+
+    def a2a_copy(m, kind, j):
         return pltpu.make_async_remote_copy(
-            src_ref=snd.at[m, j], dst_ref=rcv.at[m, my_rows, :], send_sem=a2a_send.at[m, j],
-            recv_sem=a2a_recv.at[m, me], device_id=dp_dev(target), device_id_type=MESH,
+            src_ref=snd.at[m, j, kind], dst_ref=rcv.at[m, kind, my_rows, :], send_sem=a2a_send.at[m, kind, j],
+            recv_sem=a2a_recv.at[m, kind, me], device_id=dp_dev(j), device_id_type=MESH,
         )
 
-    def a2a_own(m):
-        return pltpu.make_async_copy(snd.at[m, me], rcv.at[m, my_rows, :], loc_sem.at[m])
-
-    def project(m, k):
-        j = lax.rem(me + k, n_dp)
-        project_compute(m, j)
-
-        @pl.when(k > 0)
-        def _():
-            a2a_copy(m, j, j).start()
-
-        @pl.when(k == 0)
-        def _():
-            a2a_own(m).start()
-
-    def project_compute(m, j):
+    def a2a_in(m, kind, j):
+        at = pl.ds(pl.multiple_of(j * rows_m, rows_m), rows_m)
+        return pltpu.make_async_remote_copy(
+            src_ref=snd.at[m, j, kind], dst_ref=rcv.at[m, kind, at, :], send_sem=a2a_send.at[m, kind, j],
+            recv_sem=a2a_recv.at[m, kind, j], device_id=dp_dev(j), device_id_type=MESH,
+        )
+
+    def a2a_own(m, kind):
+        return pltpu.make_async_copy(snd.at[m, me, kind], rcv.at[m, kind, my_rows, :], loc_sem.at[m, kind])
+
+    def project(m, kinds, k, count):
+        owners = [lax.rem(me + k + i, n_dp) for i in range(count)]
+        for kind in kinds:
+            project_compute(m, kind, owners)
+        for i, j in enumerate(owners):
+            for kind in kinds:
+                @pl.when(k + i > 0)
+                def _():
+                    a2a_copy(m, kind, j).start()
+
+                @pl.when(k + i == 0)
+                def _():
+                    a2a_own(m, kind).start()
+
+    def project_compute(m, kind, owners):
         rows = pl.ds(pl.multiple_of(m * block, block), block)
-        for i in range(heads_d):
-            cols = pl.ds(pl.multiple_of(j * cols_d + i * 128, 128), 128)
-            gk = dot_tn(gs[rows, cols], q[rows, cols]) * scale
-            gv = dot_tn(p[rows, cols].astype(BF16), go[rows, cols])
-            snd[m, j, :, pl.ds(i * 128, 128)] = gk.astype(BF16)
-            snd[m, j, :, pl.ds(cols_d + i * 128, 128)] = gv.astype(BF16)
-
-    def a2a_wait(m):
-        a2a_own(m).wait()
+        outs = []
+        for j in owners:
+            for i in range(heads_d):
+                cols = pl.ds(pl.multiple_of(j * cols_d + i * 128, 128), 128)
+                if kind == 0:
+                    out = dot_tn(gs[rows, cols], q[rows, cols]) * scale
+                else:
+                    out = dot_tn(p[rows, cols].astype(BF16), go[rows, cols])
+                outs.append((j, i, out.astype(BF16)))
+        for j, i, out in outs:
+            snd[m, j, kind, :, pl.ds(i * 128, 128)] = out
+
+    def a2a_wait(m, kind):
+        a2a_own(m, kind).wait()
 
         @pl.loop(1, n_dp)
         def _(k):
-            j = lax.rem(me + k, n_dp)
-            at = pl.ds(pl.multiple_of(j * rows_m, rows_m), rows_m)
-            pltpu.make_async_remote_copy(
-                src_ref=snd.at[m, j], dst_ref=rcv.at[m, at, :], send_sem=a2a_send.at[m, j],
-                recv_sem=a2a_recv.at[m, j], device_id=dp_dev(j), device_id_type=MESH,
-            ).wait_recv()
-
-    def weight_grad(m):
-        tile = 128
+            a2a_in(m, kind, lax.rem(me + k, n_dp)).wait_recv()
+
+    def weight_grad(m, kind):
+        tile = WG_ROWS
 
         @pl.loop(0, lat_w // tile)
         def _(t):
             at = pl.ds(pl.multiple_of(t * tile, tile), tile)
-            part = dot_nn(lt_all[m, at, :], rcv[m])
+            part = dot_nn(lt_all[m, at, :], rcv[m, kind])
             if m == 0:
-                grads[at, :] = part
+                grads[kind, at, :] = part
             else:
-                grads[at, :] += part
+                grads[kind, at, :] += part
+
+    def adam(i):
+        @pl.loop(0, lat_w // ADAM_ROWS)
+        def _(t):
+            at = pl.ds(pl.multiple_of(t * ADAM_ROWS, ADAM_ROWS), ADAM_ROWS)
+            g = grads[i, at, :]
+            cur = wts[i, at, :]
+            first = 0.9 * mf[i, at, :] + 0.1 * g
+            second = 0.95 * ms[i, at, :] + 0.05 * g * g
+            new = cur - 0.02 * (first / (jnp.sqrt(second) + 1e-08) + 0.1 * cur)
+            wts[i, at, :] = new
+            wlow[i, at, :] = new.astype(BF16)
+
+    my_cols = pl.ds(pl.multiple_of(me * cols_d, cols_d), cols_d)
+
+    def kv_copy(kind, j, source):
+        cols = pl.ds(pl.multiple_of(source * cols_d, cols_d), cols_d)
+        return pltpu.make_async_remote_copy(
+            src_ref=kvs.at[kind, j], dst_ref=kv_hbm.at[kind, :, cols], send_sem=kv_send.at[kind, j],
+            recv_sem=kv_recv.at[kind, source], device_id=dp_dev(j), device_id_type=MESH,
+        )
+
+    def kv_own(kind):
+        return pltpu.make_async_copy(kvs.at[kind, me], kv_hbm.at[kind, :, my_cols], loc_sem.at[2, kind])
+
+    def next_rows(kind):
+        @pl.loop(0, n_dp // 2)
+        def _(k):
+            pair = lax.rem(me // 2 + 1 + k, n_dp // 2)
+            at = pl.ds(pl.multiple_of(pair * 2 * block, 2 * block), 2 * block)
+            out = dot_nn(nl_all[at, :], wlow[kind]).astype(BF16)
+            for i in range(2):
+                kvs[kind, 2 * pair + i] = out[i * block : (i + 1) * block, :]
+
+            @pl.when(k < n_dp // 2 - 1)
+            def _():
+                for i in range(2):
+                    kv_copy(kind, 2 * pair + i, me).start()
+
+            @pl.when(k == n_dp // 2 - 1)
+            def _():
+                kv_copy(kind, core_peer, me).start()
+                kv_own(kind).start()
+
+    def out_weights(kind):
+        return pltpu.make_async_copy(wts.at[kind], nw_hbm.at[kind], out_sem.at[2 * micro + kind])
+
+    def finish_kind(kind):
+        a2a_wait(1, kind)
+        weight_grad(1, kind)
+        adam(kind)
+        out_weights(kind).start()
+        next_rows(kind)
 
     for c in (hid_loads[0], key_loads[0]):
         c.wait()
-    prepare(0)
+
+    @pl.when(jnp.logical_not(top))
+    def _():
+        prepare(0, 0, block)
+
     val_loads[0].wait()
-    transpose_values(0)
-    for c in (hid_loads[1], key_loads[1], val_loads[1]):
-        c.wait()
+
+    def wait_rest():
+        for c in (hid_loads[1:], key_loads[1:], val_loads[1:]):
+            for d in c:
+                d.wait()
 
     @pl.when(jnp.logical_not(top))
     def _():
-        prepare(1)
-        transpose_values(1)
+        wait_rest()
+        prepare(1, 0, block)
+        for m in range(micro):
+            transpose_values(m)
 
     @pl.when(top)
     def _():
-        for c in cot_loads:
-            c.wait()
+        cot_loads[0].wait()
 
     @pl.when(early)
     def _():
         gather_second()
+
+    share = n_dp // per_micro
+    together = TOP_ROWS // CHUNK
 
     @pl.loop(0, n_chunks)
     def _(c):
-        @pl.when(jnp.logical_and(c == per_micro, top))
-        def _():
-            prepare(1)
-            transpose_values(1)
-
         @pl.when(jnp.logical_and(c == per_micro, jnp.logical_not(early)))
         def _():
             gather_second()
@@ -360,22 +465,32 @@
         def _():
             gather_third()
 
+        @pl.when(top)
+        def _():
+            @pl.when(c == per_micro)
+            def _():
+                wait_rest()
+                for d in cot_loads[1:]:
+                    d.wait()
+
+            @pl.when(lax.rem(c, together) == 0)
+            def _():
+                prepare(c // per_micro, lax.rem(c, per_micro) * CHUNK, TOP_ROWS)
+
+            chain_step(c, dot_nt)
+
         @pl.when(jnp.logical_not(top))
         def _():
             relay1(c).wait_recv()
-
-        chain_step(c)
+            chain_step(c, dot_nn)
 
         @pl.when(sec > 0)
         def _():
             relay1(c).start()
 
-        share = n_dp // per_micro
-
-        @pl.when(c >= per_micro)
-        def _():
-            for i in range(share):
-                project(0, (c - per_micro) * share + i)
+        @pl.when(jnp.logical_and(c >= per_micro, jnp.logical_not(mid)))
+        def _():
+            project(0, (1, 0), (c - per_micro) * share, share)
 
     out_first = [
         pltpu.make_async_copy(inc.at[pl.ds(m * block, block), :], ig_hbm.at[m, :, pl.ds(0, span)], out_sem.at[m])
@@ -384,86 +499,66 @@
     for c in out_first:
         c.start()
 
-    @pl.loop(0, n_dp)
-    def _(k):
-        project(1, k)
-
-    @pl.when(jnp.logical_not(early))
-    def _():
-        gather_third()
+    @pl.when(mid)
+    def _():
+        @pl.loop(0, n_dp // OWNERS)
+        def _(k):
+            project(0, (1, 0), k * OWNERS, OWNERS)
+
+    for kind in (1, 0):
+        @pl.loop(0, n_dp // OWNERS)
+        def _(k):
+            project(1, (kind,), k * OWNERS, OWNERS)
 
     @pl.when(top)
     def _():
         for c in cot2_loads:
             c.wait()
 
-    @pl.loop(0, n_chunks2 // 2)
-    def _(c):
-        second_step(c)
+    def second_steps(first, last):
+        @pl.loop(first, last)
+        def _(c):
+            second_step(c)
+
+    def forward_steps(first, last):
+        if detour:
+            @pl.when(top)
+            def _():
+                @pl.loop(first, last)
+                def _(c):
+                    relay2(c, fwd, mid_at).wait_recv()
+                    forward2(c).start()
+
+    def upto(top_at, mid_at, late_at, at):
+        bound = jnp.where(top, top_at, jnp.where(mid, mid_at, jnp.where(early, at, late_at)))
+        return bound * n_chunks2 // 16
+
+    stop0, stop1, stop2 = upto(16, 9, 7, 4), upto(16, 16, 13, 6), upto(16, 16, 16, 10)
+    second_steps(0, stop0)
+
+    @pl.when(jnp.logical_not(early))
+    def _():
+        gather_third()
 
     @pl.loop(0, n_dp // 2)
     def _(k):
         gather_wait_recv(2 * k + 1 - core)
 
-    a2a_wait(0)
-    weight_grad(0)
     for c in (w_load, mf_load, ms_load):
         c.wait()
-    a2a_wait(1)
-    weight_grad(1)
-
-    @pl.loop(0, lat_w // ADAM_ROWS)
-    def _(t):
-        at = pl.ds(pl.multiple_of(t * ADAM_ROWS, ADAM_ROWS), ADAM_ROWS)
-        for i in range(2):
-            cols = pl.ds(i * cols_d, cols_d)
-            g = grads[at, cols]
-            cur = wts[i, at, :]
-            first = 0.9 * mf[i, at, :] + 0.1 * g
-            second = 0.95 * ms[i, at, :] + 0.05 * g * g
-            new = cur - 0.02 * (first / (jnp.sqrt(second) + 1e-08) + 0.1 * cur)
-            wts[i, at, :] = new
-            wlow[at, cols] = new.astype(BF16)
-
-    out_w = pltpu.make_async_copy(wts, nw_hbm, out_sem.at[2])
-    out_w.start()
-
-    my_cols = pl.ds(pl.multiple_of(me * cols_d, cols_d), cols_d)
-
-    def kv_copy(j, source):
-        cols = pl.ds(pl.multiple_of(source * cols_d, cols_d), cols_d)
-        return pltpu.make_async_remote_copy(
-            src_ref=kvs.at[j], dst_ref=kv_hbm.at[:, :, cols], send_sem=kv_send.at[j],
-            recv_sem=kv_recv.at[source], device_id=dp_dev(j), device_id_type=MESH,
-        )
-
-    kv_own = pltpu.make_async_copy(kvs.at[me], kv_hbm.at[:, :, my_cols], loc_sem.at[2])
-
-    @pl.loop(0, n_dp // 2)
-    def _(k):
-        pair = lax.rem(me // 2 + 1 + k, n_dp // 2)
-        at = pl.ds(pl.multiple_of(pair * 2 * block, 2 * block), 2 * block)
-        out = dot_nn(nl_all[at, :], wlow[...]).astype(BF16)
-        for i in range(2):
-            for kind in range(2):
-                kvs[2 * pair + i, kind] = out[i * block : (i + 1) * block, kind * cols_d : (kind + 1) * cols_d]
-
-        @pl.when(k < n_dp // 2 - 1)
-        def _():
-            for i in range(2):
-                kv_copy(2 * pair + i, me).start()
-
-        @pl.when(k == n_dp // 2 - 1)
-        def _():
-            kv_copy(core_peer, me).start()
-            kv_own.start()
-
-    @pl.loop(n_chunks2 // 2, n_chunks2)
-    def _(c):
-        second_step(c)
+    for kind in (1, 0):
+        a2a_wait(0, kind)
+        weight_grad(0, kind)
+    second_steps(stop0, stop1)
+    forward_steps(0, n_chunks2)
+    finish_kind(1)
+    second_steps(stop1, stop2)
+    finish_kind(0)
+
+    second_steps(stop2, n_chunks2)
 
     out_second = [
-        pltpu.make_async_copy(inc2.at[pl.ds(m * block, block), :], ig_hbm.at[m, :, pl.ds(span, width - span)], out_sem.at[3 + m])
+        pltpu.make_async_copy(inc2.at[pl.ds(m * block, block), :], ig_hbm.at[m, :, pl.ds(span, width - span)], out_sem.at[micro + m])
         for m in range(micro)
     ]
     for c in out_second:
@@ -483,20 +578,25 @@
     def _(k):
         gather_wait_send(k)
 
-    for m in range(micro):
-        @pl.loop(1, n_dp)
-        def _(k):
-            j = lax.rem(me + k, n_dp)
-            a2a_copy(m, j, j).wait_send()
+    if detour:
+        @pl.when(top)
+        def _():
+            @pl.loop(0, n_chunks2)
+            def _(c):
+                forward2(c).wait_send()
 
     @pl.loop(1, n_dp)
     def _(k):
         j = lax.rem(me + k, n_dp)
-        kv_copy(j, me).wait_send()
-        kv_copy(j, j).wait_recv()
-
-    kv_own.wait()
-    out_w.wait()
+        for kind in range(2):
+            for m in range(micro):
+                a2a_copy(m, kind, j).wait_send()
+            kv_copy(kind, j, me).wait_send()
+            kv_copy(kind, j, j).wait_recv()
+
+    for kind in range(2):
+        kv_own(kind).wait()
+        out_weights(kind).wait()
     for c in out_first + out_second:
         c.wait()
 
@@ -536,6 +636,7 @@
             vmem((tokens, span), F32),
             vmem((tokens, span), BF16),
             vmem((tokens, span), BF16),
+            vmem((block, GROUP * 128), F32),
             vmem((CHUNK, span), F32),
             vmem((CHUNK, span), F32),
             vmem((tokens, 128), F32),
@@ -543,27 +644,29 @@
             vmem((micro, block, rows_m), F32),
             vmem((micro, lat_w, n_dp * rows_m), BF16),
             vmem((n_dp * block, lat_w), BF16),
-            vmem((micro, n_dp, rows_m, 2 * cols_d), BF16),
-            vmem((micro, n_dp * rows_m, 2 * cols_d), BF16),
+            vmem((micro, n_dp, 2, rows_m, cols_d), BF16),
+            vmem((micro, 2, n_dp * rows_m, cols_d), BF16),
             vmem((2, lat_w, cols_d), F32),
             vmem((2, lat_w, cols_d), F32),
             vmem((2, lat_w, cols_d), F32),
-            vmem((lat_w, 2 * cols_d), F32),
-            vmem((lat_w, 2 * cols_d), BF16),
-            vmem((n_dp, 2, block, cols_d), BF16),
+            vmem((2, lat_w, cols_d), F32),
+            vmem((2, lat_w, cols_d), BF16),
+            vmem((2, n_dp, block, cols_d), BF16),
+            vmem((tokens, width - span), BF16),
             dma((15,)),
-            dma((5,)),
+            dma((2 * micro + 2,)),
             dma((n_chunks,)),
             dma((n_chunks,)),
             dma((n_chunks2,)),
             dma((n_chunks2,)),
+            dma((n_chunks2,)),
             dma((2, 2 * n_y - 1 + n_dp // 2)),
             dma((2, n_dp)),
-            dma((micro, n_dp)),
-            dma((micro, n_dp)),
-            dma((n_dp,)),
-            dma((n_dp,)),
-            dma((3,)),
+            dma((micro, 2, n_dp)),
+            dma((micro, 2, n_dp)),
+            dma((2, n_dp)),
+            dma((2, n_dp)),
+            dma((3, 2)),
         ],
         compiler_params=pltpu.CompilerParams(
             collective_id=0, has_side_effects=True, vmem_limit_bytes=62 * 1024 * 1024

time: 228 us -> 185 us (0.81)
  Pallas kernels: 218 us -> 174 us
    pallas_call x1, Pallas kernels: 218 us -> 174 us  [body(): pl.pallas_call(functools.partial(kernel, n_sec, n_dp), out_shape=(jax.Sha...]
where the time goes in v3:
time: 185 us; the launch traced here: 184 us
  Pallas kernels  174 us (94%)
  local copies, waits for them, and re-layouts  8.24 us (4%)
    pallas_call x1, Pallas kernels, body(): pl.pallas_call(functools.partial(kernel, n_sec, n_dp), out_shape=(jax.Sha...  174 us
    unnamed x7, local copies, waits for them, and re-layouts  8.24 us

profile of v3, /device:TPU:0, one launch (start us, length us, event | category | flops | bytes accessed | tf_op | source)
XLA Modules:
  0.0 183.5 jit_solution(6147387065792550562)
XLA Ops:
  1.3 174.0 %shard_map.130 = (bf16[2,128,8192]{2,1,0:T(8,128)(2,1)}, f32[2,768,256]{2,1,0:T(8,128)}, bf16[2,128,4096]{2,1,0:T(8,128)(2,1)}) custom-call(bf16[2,128,8192]{2,1,0:T(8,128)(2,1)} %bitcast.12, bf16[2,128,4096]{2,1,0:T(8,128)(2,1)} %bitcast.14, bf16[2,128,4096]{2,1,0:T(8,128)(2,1)} %bitcast.15, bf16[2,128,768]{2,1,0:T(8,128)(2,1)} %lat_hbm.1, ...), custom_call_target="tpu_custom_call" | custom-call | tf_op jit(solution)/shard_map/pallas_call | solution.py:619
  175.3 0.0 copy-start.1
  175.3 4.8 %copy.18 = bf16[1,2,128,8192]{3,2,1,0:T(8,128)(2,1)} copy(bf16[1,2,128,8192]{3,2,1,0:T(8,128)(2,1)} %bitcast.11) | data formatting | bytes 8388608
  180.0 0.0 copy-done.1
  180.0 0.0 copy-start
  180.0 1.1 copy.19
  181.2 1.0 copy-done
  182.2 1.3 copy.20
Async XLA Ops:
  175.3 4.8 %copy-start.1 = (f32[2,768,256]{2,1,0:T(8,128)S(1)}, f32[2,768,256]{2,1,0:T(8,128)}, u32[]{:S(2)}) copy-start(f32[2,768,256]{2,1,0:T(8,128)} %get-tuple-element.7) | copy-start | bytes 4718596
  180.0 2.2 %copy-start = (bf16[2,128,4096]{2,1,0:T(8,128)(2,1)S(1)}, bf16[2,128,4096]{2,1,0:T(8,128)(2,1)}, u32[]{:S(2)}) copy-start(bf16[2,128,4096]{2,1,0:T(8,128)(2,1)} %get-tuple-element.8) | copy-start | bytes 6291460

commit v4 on v3

--- a/solution.py
+++ b/solution.py
@@ -140,63 +140,6 @@
     for m in range(micro):
         lt_all[m, :, my_rows] = jnp.transpose(lat[m].astype(F32)).astype(BF16)
 
-    others = jnp.where(sec > 0, 1, 0) + jnp.where(sec < n_sec - 1, 1, 0) + n_dp - 1
-    extra = [others]
-
-    def expect(a, b):
-        extra[0] = extra[0] + jnp.where(sec == a, 1, 0)
-
-    ring_pairs(expect)
-    pl.semaphore_wait(barrier, extra[0])
-
-    def gather_copy(slot, owner, target):
-        at = pl.ds(pl.multiple_of(owner * rows_m, rows_m), rows_m)
-        ref_l = lt_all.at[:, :, at]
-        ref_n = nl_all.at[at, :]
-        return [
-            pltpu.make_async_remote_copy(
-                src_ref=ref, dst_ref=ref, send_sem=gat_send.at[i, slot], recv_sem=gat_recv.at[i, owner],
-                device_id=dp_dev(target), device_id_type=MESH,
-            )
-            for i, ref in enumerate((ref_l, ref_n))
-        ]
-
-    def gather_start(slot, owner, target):
-        for c in gather_copy(slot, owner, target):
-            c.start()
-
-    def gather_wait_recv(owner):
-        for c in gather_copy(0, owner, me):
-            c.wait_recv()
-
-    def gather_wait_send(slot):
-        for c in gather_copy(slot, me, me):
-            c.wait_send()
-
-    x_peer = me + 2 - 4 * x_lo
-    core_peer = me + 1 - 2 * core
-
-    def y_peer(dy):
-        return lax.rem(y_at + dy, n_y) * 4 + x_lo * 2 + core
-
-    gather_start(0, me, x_peer)
-    for dy in range(1, n_y):
-        gather_start(dy, me, y_peer(dy))
-
-    def gather_second():
-        gather_wait_recv(x_peer)
-        for dy in range(1, n_y):
-            gather_start(n_y - 1 + dy, x_peer, y_peer(dy))
-
-    def gather_third():
-        for dy in range(1, n_y):
-            gather_wait_recv(y_peer(dy))
-            gather_wait_recv(y_peer(dy) + 2 - 4 * x_lo)
-
-        @pl.loop(0, n_dp // 2)
-        def _(k):
-            gather_start(2 * n_y - 1 + k, 2 * k + core, core_peer)
-
     def prepare(m, start, count):
         @pl.loop(0, count // NORM_ROWS)
         def _(t):
@@ -226,6 +169,85 @@
                 s = jnp.where(allowed, sbuf[pl.ds(0, count), pl.ds(j * 128, 128)] * scale, -1e30)
                 e = jnp.exp(s - jnp.max(s, axis=1, keepdims=True))
                 p[rows, cols] = e / jnp.sum(e, axis=1, keepdims=True)
+
+    @pl.when(top)
+    def _():
+        hid_loads[0].wait()
+        key_loads[0].wait()
+        prepare(0, 0, TOP_ROWS)
+
+    others = jnp.where(sec > 0, 1, 0) + jnp.where(sec < n_sec - 1, 1, 0) + n_dp - 1
+    extra = [others]
+
+    def expect(a, b):
+        extra[0] = extra[0] + jnp.where(sec == a, 1, 0)
+
+    ring_pairs(expect)
+    pl.semaphore_wait(barrier, extra[0])
+
+    def gather_copy(slot, owner, target):
+        at = pl.ds(pl.multiple_of(owner * rows_m, rows_m), rows_m)
+        ref_l = lt_all.at[:, :, at]
+        ref_n = nl_all.at[at, :]
+        return [
+            pltpu.make_async_remote_copy(
+                src_ref=ref, dst_ref=ref, send_sem=gat_send.at[i, slot], recv_sem=gat_recv.at[i, owner],
+                device_id=dp_dev(target), device_id_type=MESH,
+            )
+            for i, ref in enumerate((ref_l, ref_n))
+        ]
+
+    def gather_start(slot, owner, target):
+        for c in gather_copy(slot, owner, target):
+            c.start()
+
+    def gather_wait_recv(owner):
+        for c in gather_copy(0, owner, me):
+            c.wait_recv()
+
+    def gather_wait_send(slot):
+        for c in gather_copy(slot, me, me):
+            c.wait_send()
+
+    x_peer = me + 2 - 4 * x_lo
+    core_peer = me + 1 - 2 * core
+
+    def y_peer(dy):
+        return lax.rem(y_at + dy, n_y) * 4 + x_lo * 2 + core
+
+    def beside(j):
+        return j + 2 - 4 * x_lo
+
+    near = sorted({1, n_y - 1} - {0})
+    far = [2] if n_y == 4 else []
+
+    gather_start(0, me, x_peer)
+    for dy in near:
+        gather_start(dy, me, y_peer(dy))
+
+    def gather_second():
+        gather_wait_recv(x_peer)
+        for dy in near:
+            gather_start(n_y - 1 + dy, x_peer, y_peer(dy))
+
+    def gather_core(owner):
+        gather_start(2 * n_y - 1 + owner // 2, owner, core_peer)
+
+    def gather_third():
+        for dy in near:
+            gather_wait_recv(y_peer(dy))
+            gather_wait_recv(beside(y_peer(dy)))
+        for dy in far:
+            gather_start(dy, y_peer(n_y - 1), y_peer(1))
+            gather_start(n_y - 1 + dy, beside(y_peer(1)), y_peer(n_y - 1))
+        for owner in [me, x_peer] + [y_peer(dy) for dy in near] + [beside(y_peer(dy)) for dy in near]:
+            gather_core(owner)
+
+    def gather_fourth():
+        for dy in far:
+            for owner in (y_peer(dy), beside(y_peer(dy))):
+                gather_wait_recv(owner)
+                gather_core(owner)
 
     def transpose_values(m):
         @pl.loop(0, heads // 4)
@@ -323,17 +345,28 @@
     def a2a_own(m, kind):
         return pltpu.make_async_copy(snd.at[m, me, kind], rcv.at[m, kind, my_rows, :], loc_sem.at[m, kind])
 
-    def project(m, kinds, k, count):
-        owners = [lax.rem(me + k + i, n_dp) for i in range(count)]
+    def owner_at(g, i):
+        if n_y == 4 and OWNERS == 4:
+            odd, high = lax.rem(g, 2), g // 2
+            dy = (2 * g + 1, 15 - 2 * g, 2, 0)[i]
+            dx = (0, 1, 1 - odd, 1 - high)[i]
+            dc = (high, 1 - high, lax.rem(odd + high, 2), 1 - odd)[i]
+            return lax.rem(y_at + dy, 4) * 4 + lax.rem(x_lo + dx, 2) * 2 + lax.rem(core + dc, 2)
+        return lax.rem(me + 1 + OWNERS * g + i, n_dp)
+
+    def project(m, kinds, g):
+        owners = [owner_at(g, i) for i in range(OWNERS)]
         for kind in kinds:
             project_compute(m, kind, owners)
         for i, j in enumerate(owners):
             for kind in kinds:
-                @pl.when(k + i > 0)
+                own = OWNERS * g + i == n_dp - 1
+
+                @pl.when(jnp.logical_not(own))
                 def _():
                     a2a_copy(m, kind, j).start()
 
-                @pl.when(k + i == 0)
+                @pl.when(own)
                 def _():
                     a2a_own(m, kind).start()
 
@@ -394,7 +427,7 @@
     def kv_own(kind):
         return pltpu.make_async_copy(kvs.at[kind, me], kv_hbm.at[kind, :, my_cols], loc_sem.at[2, kind])
 
-    def next_rows(kind):
+    def next_rows(kind, send):
         @pl.loop(0, n_dp // 2)
         def _(k):
             pair = lax.rem(me // 2 + 1 + k, n_dp // 2)
@@ -402,32 +435,39 @@
             out = dot_nn(nl_all[at, :], wlow[kind]).astype(BF16)
             for i in range(2):
                 kvs[kind, 2 * pair + i] = out[i * block : (i + 1) * block, :]
-
-            @pl.when(k < n_dp // 2 - 1)
-            def _():
-                for i in range(2):
-                    kv_copy(kind, 2 * pair + i, me).start()
-
-            @pl.when(k == n_dp // 2 - 1)
-            def _():
-                kv_copy(kind, core_peer, me).start()
-                kv_own(kind).start()
+            if send:
+                send_rows(kind, k)
+
+    def send_rows(kind, k):
+        pair = lax.rem(me // 2 + 1 + k, n_dp // 2)
+
+        @pl.when(k < n_dp // 2 - 1)
+        def _():
+            for i in range(2):
+                kv_copy(kind, 2 * pair + i, me).start()
+
+        @pl.when(k == n_dp // 2 - 1)
+        def _():
+            kv_copy(kind, core_peer, me).start()
+            kv_own(kind).start()
 
     def out_weights(kind):
         return pltpu.make_async_copy(wts.at[kind], nw_hbm.at[kind], out_sem.at[2 * micro + kind])
 
-    def finish_kind(kind):
+    def update_kind(kind):
         a2a_wait(1, kind)
         weight_grad(1, kind)
         adam(kind)
         out_weights(kind).start()
-        next_rows(kind)
-
-    for c in (hid_loads[0], key_loads[0]):
-        c.wait()
+
+    def finish_kind(kind):
+        update_kind(kind)
+        next_rows(kind, True)
 
     @pl.when(jnp.logical_not(top))
     def _():
+        hid_loads[0].wait()
+        key_loads[0].wait()
         prepare(0, 0, block)
 
     val_loads[0].wait()
@@ -448,22 +488,29 @@
     def _():
         cot_loads[0].wait()
 
-    @pl.when(early)
+    soon = sec < n_sec - 2
+
+    @pl.when(soon)
     def _():
         gather_second()
 
-    share = n_dp // per_micro
     together = TOP_ROWS // CHUNK
 
     @pl.loop(0, n_chunks)
     def _(c):
-        @pl.when(jnp.logical_and(c == per_micro, jnp.logical_not(early)))
+        @pl.when(jnp.logical_and(c == per_micro // 2, jnp.logical_not(soon)))
         def _():
             gather_second()
 
+        third_at = jnp.where(early, per_micro // 2, per_micro + per_micro // 2)
+
+        @pl.when(jnp.logical_and(c == third_at, jnp.logical_not(top)))
+        def _():
+            gather_third()
+
         @pl.when(jnp.logical_and(c == per_micro + per_micro // 2, early))
         def _():
-            gather_third()
+            gather_fourth()
 
         @pl.when(top)
         def _():
@@ -473,7 +520,7 @@
                 for d in cot_loads[1:]:
                     d.wait()
 
-            @pl.when(lax.rem(c, together) == 0)
+            @pl.when(jnp.logical_and(lax.rem(c, together) == 0, c > 0))
             def _():
                 prepare(c // per_micro, lax.rem(c, per_micro) * CHUNK, TOP_ROWS)
 
@@ -488,9 +535,11 @@
         def _():
             relay1(c).start()
 
-        @pl.when(jnp.logical_and(c >= per_micro, jnp.logical_not(mid)))
-        def _():
-            project(0, (1, 0), (c - per_micro) * share, share)
+        project_now = jnp.logical_and(c >= per_micro, c < per_micro + n_dp // OWNERS)
+
+        @pl.when(jnp.logical_and(project_now, jnp.logical_not(mid)))
+        def _():
+            project(0, (1, 0), c - per_micro)
 
     out_first = [
         pltpu.make_async_copy(inc.at[pl.ds(m * block, block), :], ig_hbm.at[m, :, pl.ds(0, span)], out_sem.at[m])
@@ -503,12 +552,12 @@
     def _():
         @pl.loop(0, n_dp // OWNERS)
         def _(k):
-            project(0, (1, 0), k * OWNERS, OWNERS)
+            project(0, (1, 0), k)
 
     for kind in (1, 0):
         @pl.loop(0, n_dp // OWNERS)
         def _(k):
-            project(1, (kind,), k * OWNERS, OWNERS)
+            project(1, (kind,), k)
 
     @pl.when(top)
     def _():
@@ -529,16 +578,25 @@
                     relay2(c, fwd, mid_at).wait_recv()
                     forward2(c).start()
 
-    def upto(top_at, mid_at, late_at, at):
-        bound = jnp.where(top, top_at, jnp.where(mid, mid_at, jnp.where(early, at, late_at)))
-        return bound * n_chunks2 // 16
-
-    stop0, stop1, stop2 = upto(16, 9, 7, 4), upto(16, 16, 13, 6), upto(16, 16, 16, 10)
-    second_steps(0, stop0)
+    def upto(late_at, early_at):
+        return jnp.where(top, n_chunks2, jnp.where(early, early_at, late_at) * n_chunks2 // 16)
+
+    stops = [0, upto(7, 0), upto(13, 1), upto(16, 3), upto(16, 7), n_chunks2]
+    second_steps(stops[0], stops[1])
+
+    @pl.when(top)
+    def _():
+        gather_third()
+
+    forward_steps(0, n_chunks2 // 4)
 
     @pl.when(jnp.logical_not(early))
     def _():
-        gather_third()
+        gather_fourth()
+
+    second_steps(stops[1], stops[2])
+    half = n_chunks2 // 2
+    forward_steps(n_chunks2 // 4, half)
 
     @pl.loop(0, n_dp // 2)
     def _(k):
@@ -546,16 +604,39 @@
 
     for c in (w_load, mf_load, ms_load):
         c.wait()
-    for kind in (1, 0):
+
+    def part_grads(kind):
         a2a_wait(0, kind)
         weight_grad(0, kind)
-    second_steps(stop0, stop1)
-    forward_steps(0, n_chunks2)
-    finish_kind(1)
-    second_steps(stop1, stop2)
-    finish_kind(0)
-
-    second_steps(stop2, n_chunks2)
+
+    @pl.when(top)
+    def _():
+        pieces = [
+            lambda: part_grads(1),
+            lambda: part_grads(0),
+            lambda: update_kind(1),
+            lambda: next_rows(1, False),
+            lambda: update_kind(0),
+            lambda: next_rows(0, False),
+        ]
+        left = n_chunks2 - half
+        for i, piece in enumerate(pieces):
+            forward_steps(half + i * left // len(pieces), half + (i + 1) * left // len(pieces))
+            piece()
+        for kind in (1, 0):
+            @pl.loop(0, n_dp // 2)
+            def _(k):
+                send_rows(kind, k)
+
+    @pl.when(jnp.logical_not(top))
+    def _():
+        part_grads(1)
+        part_grads(0)
+        second_steps(stops[2], stops[3])
+        finish_kind(1)
+        second_steps(stops[3], stops[4])
+        finish_kind(0)
+        second_steps(stops[4], stops[5])
 
     out_second = [
         pltpu.make_async_copy(inc2.at[pl.ds(m * block, block), :], ig_hbm.at[m, :, pl.ds(span, width - span)], out_sem.at[micro + m])

time: 185 us -> 168 us (0.908)
  Pallas kernels: 174 us -> 158 us
    pallas_call x1, Pallas kernels: 174 us -> 158 us  [body(): pl.pallas_call(functools.partial(kernel, n_sec, n_dp), out_shape=(jax.Sha...]
where the time goes in v4:
time: 168 us
  Pallas kernels  158 us (94%)
  local copies, waits for them, and re-layouts  8.24 us (5%)
    pallas_call x1, Pallas kernels, body(): pl.pallas_call(functools.partial(kernel, n_sec, n_dp), out_shape=(jax.Sha...  158 us
    unnamed x7, local copies, waits for them, and re-layouts  8.24 us

profile of v4, /device:TPU:0, one launch (start us, length us, event | category | flops | bytes accessed | tf_op | source)
XLA Modules:
  0.0 167.8 jit_solution(13602798024795829026)
XLA Ops:
  1.3 158.3 %shard_map.130 = (bf16[2,128,8192]{2,1,0:T(8,128)(2,1)}, f32[2,768,256]{2,1,0:T(8,128)}, bf16[2,128,4096]{2,1,0:T(8,128)(2,1)}) custom-call(bf16[2,128,8192]{2,1,0:T(8,128)(2,1)} %bitcast.12, bf16[2,128,4096]{2,1,0:T(8,128)(2,1)} %bitcast.14, bf16[2,128,4096]{2,1,0:T(8,128)(2,1)} %bitcast.15, bf16[2,128,768]{2,1,0:T(8,128)(2,1)} %lat_hbm.1, ...), custom_call_target="tpu_custom_call" | custom-call | tf_op jit(solution)/shard_map/pallas_call | solution.py:700
  159.6 0.0 copy-start.1
  159.6 4.8 %copy.18 = bf16[1,2,128,8192]{3,2,1,0:T(8,128)(2,1)} copy(bf16[1,2,128,8192]{3,2,1,0:T(8,128)(2,1)} %bitcast.11) | data formatting | bytes 8388608
  164.3 0.0 copy-done.1
  164.3 0.0 copy-start
  164.3 1.1 copy.19
  165.5 1.0 copy-done
  166.5 1.3 copy.20
Async XLA Ops:
  159.6 4.8 %copy-start.1 = (f32[2,768,256]{2,1,0:T(8,128)S(1)}, f32[2,768,256]{2,1,0:T(8,128)}, u32[]{:S(2)}) copy-start(f32[2,768,256]{2,1,0:T(8,128)} %get-tuple-element.7) | copy-start | bytes 4718596
  164.3 2.2 %copy-start = (bf16[2,128,4096]{2,1,0:T(8,128)(2,1)S(1)}, bf16[2,128,4096]{2,1,0:T(8,128)(2,1)}, u32[]{:S(2)}) copy-start(bf16[2,128,4096]{2,1,0:T(8,128)(2,1)} %get-tuple-element.8) | copy-start | bytes 6291460

commit v5 on v4

--- a/solution.py
+++ b/solution.py
@@ -18,6 +18,7 @@
 GROUP = 8
 ADAM_ROWS = 64
 WG_ROWS = 256
+LIMIT = 54 * 1024 * 1024
 F32 = jnp.float32
 BF16 = jnp.bfloat16
 MESH = pl.DeviceIdType.MESH
@@ -38,10 +39,10 @@
 def kernel(
     n_sec, n_dp,
     hid_hbm, key_hbm, val_hbm, lat_hbm, nl_hbm, media_ref, cot_hbm, gate_ref, w_hbm, mf_hbm, ms_hbm,
-    ig_hbm, nw_hbm, kv_hbm,
-    hid, keys, vals, lat, inc, inc2, q, p, go, gs, sbuf, gpbuf, gbuf, rinv, coef, maskf,
-    lt_all, nl_all, snd, rcv, wts, mf, ms, grads, wlow, kvs, fwd,
-    in_sem, out_sem, r1_send, r1_recv, r2_send, r2_recv,
+    inc, inc2, wts, kv,
+    hid, keys, vals, lat, q, p, go, gs, sbuf, gpbuf, gbuf, rinv, coef, maskf,
+    lt_all, nl_all, snd, rcv, mf, ms, grads, wlow, kvs, fwd,
+    in_sem, r1_send, r1_recv, r2_send, r2_recv,
     f_send, gat_send, gat_recv, a2a_send, a2a_recv, kv_send, kv_recv, loc_sem,
 ):
     sec, me = lax.axis_index("section"), lax.axis_index("dp")
@@ -420,12 +421,12 @@
     def kv_copy(kind, j, source):
         cols = pl.ds(pl.multiple_of(source * cols_d, cols_d), cols_d)
         return pltpu.make_async_remote_copy(
-            src_ref=kvs.at[kind, j], dst_ref=kv_hbm.at[kind, :, cols], send_sem=kv_send.at[kind, j],
+            src_ref=kvs.at[kind, j], dst_ref=kv.at[kind, :, cols], send_sem=kv_send.at[kind, j],
             recv_sem=kv_recv.at[kind, source], device_id=dp_dev(j), device_id_type=MESH,
         )
 
     def kv_own(kind):
-        return pltpu.make_async_copy(kvs.at[kind, me], kv_hbm.at[kind, :, my_cols], loc_sem.at[2, kind])
+        return pltpu.make_async_copy(kvs.at[kind, me], kv.at[kind, :, my_cols], loc_sem.at[2, kind])
 
     def next_rows(kind, send):
         @pl.loop(0, n_dp // 2)
@@ -451,14 +452,10 @@
             kv_copy(kind, core_peer, me).start()
             kv_own(kind).start()
 
-    def out_weights(kind):
-        return pltpu.make_async_copy(wts.at[kind], nw_hbm.at[kind], out_sem.at[2 * micro + kind])
-
     def update_kind(kind):
         a2a_wait(1, kind)
         weight_grad(1, kind)
         adam(kind)
-        out_weights(kind).start()
 
     def finish_kind(kind):
         update_kind(kind)
@@ -540,13 +537,6 @@
         @pl.when(jnp.logical_and(project_now, jnp.logical_not(mid)))
         def _():
             project(0, (1, 0), c - per_micro)
-
-    out_first = [
-        pltpu.make_async_copy(inc.at[pl.ds(m * block, block), :], ig_hbm.at[m, :, pl.ds(0, span)], out_sem.at[m])
-        for m in range(micro)
-    ]
-    for c in out_first:
-        c.start()
 
     @pl.when(mid)
     def _():
@@ -638,13 +628,6 @@
         finish_kind(0)
         second_steps(stops[4], stops[5])
 
-    out_second = [
-        pltpu.make_async_copy(inc2.at[pl.ds(m * block, block), :], ig_hbm.at[m, :, pl.ds(span, width - span)], out_sem.at[micro + m])
-        for m in range(micro)
-    ]
-    for c in out_second:
-        c.start()
-
     @pl.when(sec > 0)
     def _():
         @pl.loop(0, n_chunks)
@@ -677,8 +660,20 @@
 
     for kind in range(2):
         kv_own(kind).wait()
-        out_weights(kind).wait()
-    for c in out_first + out_second:
+
+
+def store(inc, inc2, wts, kv, ig_hbm, nw_hbm, kv_hbm, sem):
+    _, micro, block, width = ig_hbm.shape
+    span = inc.shape[1]
+    pairs = [(wts, nw_hbm.at[0]), (kv, kv_hbm.at[0])]
+    for m in range(micro):
+        rows = pl.ds(m * block, block)
+        pairs.append((inc.at[rows, :], ig_hbm.at[0, m, :, pl.ds(0, span)]))
+        pairs.append((inc2.at[rows, :], ig_hbm.at[0, m, :, pl.ds(span, width - span)]))
+    copies = [pltpu.make_async_copy(src, dst, sem.at[i]) for i, (src, dst) in enumerate(pairs)]
+    for c in copies:
+        c.start()
+    for c in copies:
         c.wait()
 
 
@@ -697,22 +692,21 @@
     vmem_spec = pl.BlockSpec(memory_space=pltpu.VMEM)
     dma = pltpu.SemaphoreType.DMA
     vmem = pltpu.VMEM
-    grad_in, new_w, kv = pl.pallas_call(
+    held = pl.pallas_call(
         functools.partial(kernel, n_sec, n_dp),
         out_shape=(
-            jax.ShapeDtypeStruct((micro, block, width), BF16),
-            jax.ShapeDtypeStruct((2, lat_w, cols_d), F32),
-            jax.ShapeDtypeStruct((2, rows_m, span), BF16),
+            vmem((tokens, span), BF16),
+            vmem((tokens, width - span), BF16),
+            vmem((2, lat_w, cols_d), F32),
+            vmem((2, rows_m, span), BF16),
         ),
         in_specs=[any_spec] * 5 + [vmem_spec, any_spec, vmem_spec] + [any_spec] * 3,
-        out_specs=(any_spec, any_spec, any_spec),
+        out_specs=(vmem_spec,) * 4,
         scratch_shapes=[
             vmem((tokens, width), BF16),
             vmem((micro, rows_m, span), BF16),
             vmem((micro, rows_m, span), BF16),
             vmem((micro, rows_m, lat_w), BF16),
-            vmem((tokens, span), BF16),
-            vmem((tokens, width - span), BF16),
             vmem((tokens, span), BF16),
             vmem((tokens, span), F32),
             vmem((tokens, span), BF16),
@@ -730,12 +724,10 @@
             vmem((2, lat_w, cols_d), F32),
             vmem((2, lat_w, cols_d), F32),
             vmem((2, lat_w, cols_d), F32),
-            vmem((2, lat_w, cols_d), F32),
             vmem((2, lat_w, cols_d), BF16),
             vmem((2, n_dp, block, cols_d), BF16),
             vmem((tokens, width - span), BF16),
             dma((15,)),
-            dma((2 * micro + 2,)),
             dma((n_chunks,)),
             dma((n_chunks,)),
             dma((n_chunks2,)),
@@ -750,13 +742,25 @@
             dma((3, 2)),
         ],
         compiler_params=pltpu.CompilerParams(
-            collective_id=0, has_side_effects=True, vmem_limit_bytes=62 * 1024 * 1024
+            collective_id=0, has_side_effects=True, vmem_limit_bytes=LIMIT
         ),
     )(
         hidden_states[0], key_rows[0], value_rows[0], latents, next_latents, media_index, cotangent,
         gate_alpha.reshape(1, 1), weights[0], moment_first[0], moment_second[0],
     )
-    return grad_in[None], new_w[None], kv[None]
+    grad_in, new_w, kv = pl.pallas_call(
+        store,
+        out_shape=(
+            jax.ShapeDtypeStruct((1, micro, block, width), BF16),
+            jax.ShapeDtypeStruct((1, 2, lat_w, cols_d), F32),
+            jax.ShapeDtypeStruct((1, 2, rows_m, span), BF16),
+        ),
+        in_specs=[vmem_spec] * 4,
+        out_specs=(any_spec, any_spec, any_spec),
+        scratch_shapes=[dma((2 + 2 * micro,))],
+        compiler_params=pltpu.CompilerParams(vmem_limit_bytes=1024 * 1024),
+    )(*held)
+    return grad_in, new_w, kv
 
 
 def solution(mesh):

time: 168 us -> 163 us (0.970)
  local copies, waits for them, and re-layouts: 8.24 us -> 0 us
  Pallas kernels: 158 us -> 160 us
    unnamed x7 -> x0, local copies, waits for them, and re-layouts: 8.24 us -> none
    pallas_call x1 -> x2, Pallas kernels: 158 us -> 160 us  [the longest x1 157 us: body(): pl.pallas_call(functools.partial(kernel, n_sec, n_dp), out_shape=(vmem((t...]
where the time goes in v5:
time: 163 us; the launch traced here: 162 us
  Pallas kernels  160 us (98%)
    pallas_call x1, Pallas kernels, body(): pl.pallas_call(functools.partial(kernel, n_sec, n_dp), out_shape=(vmem((t...  157 us

profile of v5, /device:TPU:0, one launch (start us, length us, event | category | flops | bytes accessed | tf_op | source)
XLA Modules:
  0.0 161.5 jit_solution(7496458066702509333)
XLA Ops:
  1.3 157.0 %shard_map.130 = (bf16[256,4096]{1,0:T(8,128)(2,1)S(1)}, bf16[256,4096]{1,0:T(8,128)(2,1)S(1)}, f32[2,768,256]{2,1,0:T(8,128)S(1)}, bf16[2,128,4096]{2,1,0:T(8,128)(2,1)S(1)}) custom-call(bf16[2,128,8192]{2,1,0:T(8,128)(2,1)} %bitcast.8, bf16[2,128,4096]{2,1,0:T(8,128)(2,1)} %bitcast.9, bf16[2,128,4096]{2,1,0:T(8,128)(2,1)} %bitcast.10, ...), custom_call_target="tpu_custom_call" | custom-call | tf_op jit(solution)/shard_map/pallas_call | solution.py:695
  158.3 3.2 %shard_map.131 = (bf16[1,2,128,8192]{3,2,1,0:T(8,128)(2,1)}, f32[1,2,768,256]{3,2,1,0:T(8,128)}, bf16[1,2,128,4096]{3,2,1,0:T(8,128)(2,1)}) custom-call(bf16[256,4096]{1,0:T(8,128)(2,1)S(1)} %get-tuple-element.7.inc, bf16[256,4096]{1,0:T(8,128)(2,1)S(1)} %get-tuple-element.8.inc2, f32[2,768,256]{2,1,0:T(8,128)S(1)} %get-tuple-element.9.wts, ...), custom_call_target="tpu_custom_call" | custom-call | tf_op jit(solution)/shard_map/pallas_call | solution.py:751

commit v6 on v5

--- a/solution.py
+++ b/solution.py
@@ -11,7 +11,7 @@
 HEAD_DIM = 128
 LATENTS = 64
 CHUNK = 16
-CHUNK2 = 16
+SPLIT2 = 2
 NORM_ROWS = 16
 TOP_ROWS = 32
 OWNERS = 4
@@ -56,7 +56,7 @@
     tokens = micro * block
     n_chunks = tokens // CHUNK
     per_micro = n_chunks // micro
-    n_chunks2 = tokens // CHUNK2
+    n_chunks2 = n_chunks * SPLIT2
     n_y = n_dp // 4
     scale = 1.0 / math.sqrt(HEAD_DIM)
     core = lax.rem(me, 2)
@@ -156,9 +156,9 @@
                 cols = pl.ds(c * 128, 128)
                 q[rows, cols] = (hid[rows, cols].astype(F32) * r).astype(BF16)
 
-        rows = pl.ds(pl.multiple_of(m * block + start, count), count)
+        rows = pl.ds(m * block + start, count)
         half = lax.broadcasted_iota(jnp.int32, (count, rows_m), 1) // LATENTS
-        allowed = half.astype(F32) == maskf[m, pl.ds(pl.multiple_of(start, count), count), :]
+        allowed = half.astype(F32) == maskf[m, pl.ds(start, count), :]
 
         @pl.loop(0, heads // GROUP)
         def _(hg):
@@ -264,17 +264,23 @@
             device_id=(jnp.maximum(sec - 1, 0), me), device_id_type=MESH,
         )
 
+    part2 = (width - span) // SPLIT2
+
+    def at2(ref, c):
+        return ref.at[
+            pl.ds(pl.multiple_of(c // SPLIT2 * CHUNK, CHUNK), CHUNK),
+            pl.ds(pl.multiple_of(lax.rem(c, SPLIT2) * part2, 128), part2),
+        ]
+
     def relay2(c, dst=inc2, to=None):
-        rows = pl.ds(pl.multiple_of(c * CHUNK2, CHUNK2), CHUNK2)
         return pltpu.make_async_remote_copy(
-            src_ref=inc2.at[rows, :], dst_ref=dst.at[rows, :], send_sem=r2_send.at[c], recv_sem=r2_recv.at[c],
+            src_ref=at2(inc2, c), dst_ref=at2(dst, c), send_sem=r2_send.at[c], recv_sem=r2_recv.at[c],
             device_id=(jnp.maximum(sec - 1, 0) if to is None else to, me), device_id_type=MESH,
         )
 
     def forward2(c):
-        rows = pl.ds(pl.multiple_of(c * CHUNK2, CHUNK2), CHUNK2)
         return pltpu.make_async_remote_copy(
-            src_ref=fwd.at[rows, :], dst_ref=inc2.at[rows, :], send_sem=f_send.at[c], recv_sem=r2_recv.at[c],
+            src_ref=at2(fwd, c), dst_ref=at2(inc2, c), send_sem=f_send.at[c], recv_sem=r2_recv.at[c],
             device_id=(mid_at - 1, me), device_id_type=MESH,
         )
 
@@ -314,12 +320,12 @@
         def _():
             relay2(c).wait_recv()
 
-        for t in range(CHUNK2 // 16):
-            rows = pl.ds(pl.multiple_of(c * CHUNK2 + t * 16, 16), 16)
-            b = coef[rows, :]
-            for h in range((width - span) // 128):
-                cols, hcols = pl.ds(h * 128, 128), pl.ds(span + h * 128, 128)
-                inc2[rows, cols] = (inc2[rows, cols].astype(F32) - b * hid[rows, hcols].astype(F32)).astype(BF16)
+        rows = pl.ds(pl.multiple_of(c // SPLIT2 * CHUNK, CHUNK), CHUNK)
+        b = coef[rows, :]
+        for h in range(part2 // 128):
+            cols = pl.ds(pl.multiple_of(lax.rem(c, SPLIT2) * part2 + h * 128, 128), 128)
+            hcols = pl.ds(pl.multiple_of(span + lax.rem(c, SPLIT2) * part2 + h * 128, 128), 128)
+            inc2[rows, cols] = (inc2[rows, cols].astype(F32) - b * hid[rows, hcols].astype(F32)).astype(BF16)
 
         @pl.when(jnp.logical_and(sec > 0, jnp.logical_not(mid)))
         def _():
@@ -457,10 +463,6 @@
         weight_grad(1, kind)
         adam(kind)
 
-    def finish_kind(kind):
-        update_kind(kind)
-        next_rows(kind, True)
-
     @pl.when(jnp.logical_not(top))
     def _():
         hid_loads[0].wait()
@@ -491,7 +493,6 @@
     def _():
         gather_second()
 
-    together = TOP_ROWS // CHUNK
 
     @pl.loop(0, n_chunks)
     def _(c):
@@ -499,7 +500,7 @@
         def _():
             gather_second()
 
-        third_at = jnp.where(early, per_micro // 2, per_micro + per_micro // 2)
+        third_at = jnp.where(early, per_micro // 2, per_micro + per_micro // 4)
 
         @pl.when(jnp.logical_and(c == third_at, jnp.logical_not(top)))
         def _():
@@ -517,9 +518,13 @@
                 for d in cot_loads[1:]:
                     d.wait()
 
-            @pl.when(jnp.logical_and(lax.rem(c, together) == 0, c > 0))
+            @pl.when(c == TOP_ROWS // CHUNK)
             def _():
-                prepare(c // per_micro, lax.rem(c, per_micro) * CHUNK, TOP_ROWS)
+                prepare(0, TOP_ROWS, block - TOP_ROWS)
+
+            @pl.when(c == per_micro)
+            def _():
+                prepare(1, 0, block)
 
             chain_step(c, dot_nt)
 
@@ -561,46 +566,32 @@
 
     def forward_steps(first, last):
         if detour:
-            @pl.when(top)
-            def _():
-                @pl.loop(first, last)
-                def _(c):
-                    relay2(c, fwd, mid_at).wait_recv()
-                    forward2(c).start()
-
-    def upto(late_at, early_at):
-        return jnp.where(top, n_chunks2, jnp.where(early, early_at, late_at) * n_chunks2 // 16)
-
-    stops = [0, upto(7, 0), upto(13, 1), upto(16, 3), upto(16, 7), n_chunks2]
-    second_steps(stops[0], stops[1])
-
-    @pl.when(top)
-    def _():
-        gather_third()
-
-    forward_steps(0, n_chunks2 // 4)
-
-    @pl.when(jnp.logical_not(early))
-    def _():
-        gather_fourth()
-
-    second_steps(stops[1], stops[2])
-    half = n_chunks2 // 2
-    forward_steps(n_chunks2 // 4, half)
-
-    @pl.loop(0, n_dp // 2)
-    def _(k):
-        gather_wait_recv(2 * k + 1 - core)
-
-    for c in (w_load, mf_load, ms_load):
-        c.wait()
+            @pl.loop(first, last)
+            def _(c):
+                relay2(c, fwd, mid_at).wait_recv()
+                forward2(c).start()
 
     def part_grads(kind):
         a2a_wait(0, kind)
         weight_grad(0, kind)
 
+    def gather_end():
+        @pl.loop(0, n_dp // 2)
+        def _(k):
+            gather_wait_recv(2 * k + 1 - core)
+
+        for c in (w_load, mf_load, ms_load):
+            c.wait()
+
     @pl.when(top)
     def _():
+        second_steps(0, n_chunks2)
+        gather_third()
+        quarter = n_chunks2 // 4
+        forward_steps(0, quarter)
+        gather_fourth()
+        forward_steps(quarter, 2 * quarter)
+        gather_end()
         pieces = [
             lambda: part_grads(1),
             lambda: part_grads(0),
@@ -609,9 +600,9 @@
             lambda: update_kind(0),
             lambda: next_rows(0, False),
         ]
-        left = n_chunks2 - half
+        left = n_chunks2 - 2 * quarter
         for i, piece in enumerate(pieces):
-            forward_steps(half + i * left // len(pieces), half + (i + 1) * left // len(pieces))
+            forward_steps(2 * quarter + i * left // len(pieces), 2 * quarter + (i + 1) * left // len(pieces))
             piece()
         for kind in (1, 0):
             @pl.loop(0, n_dp // 2)
@@ -620,13 +611,28 @@
 
     @pl.when(jnp.logical_not(top))
     def _():
-        part_grads(1)
-        part_grads(0)
-        second_steps(stops[2], stops[3])
-        finish_kind(1)
-        second_steps(stops[3], stops[4])
-        finish_kind(0)
-        second_steps(stops[4], stops[5])
+        def gather_rest():
+            @pl.when(jnp.logical_not(early))
+            def _():
+                gather_fourth()
+
+        pieces = [
+            (gather_rest, 0, 10, 12),
+            (gather_end, 0, 13, 15),
+            (lambda: part_grads(1), 0, 13, 15),
+            (lambda: part_grads(0), 0, 14, 16),
+            (lambda: update_kind(1), jnp.where(sec > 0, 3 + sec, 0), 16, 16),
+            (lambda: next_rows(1, True), jnp.where(sec > 0, 4 + sec, 0), 16, 16),
+            (lambda: update_kind(0), jnp.where(sec > 0, 7 + 2 * sec, 0), 16, 16),
+            (lambda: next_rows(0, True), jnp.where(sec > 0, 8 + 2 * sec, 0), 16, 16),
+        ]
+        done = 0
+        for piece, low, at_mid, high in pieces:
+            until = jnp.where(early, low, jnp.where(mid, at_mid, high)) * n_chunks2 // 16
+            second_steps(done, until)
+            done = until
+            piece()
+        second_steps(done, n_chunks2)
 
     @pl.when(sec > 0)
     def _():
@@ -687,7 +693,8 @@
     lat_w, cols_d = weights.shape[2], weights.shape[3]
     tokens = micro * block
     n_y = n_dp // 4
-    n_chunks, n_chunks2 = tokens // CHUNK, tokens // CHUNK2
+    n_chunks = tokens // CHUNK
+    n_chunks2 = n_chunks * SPLIT2
     any_spec = pl.BlockSpec(memory_space=pl.ANY)
     vmem_spec = pl.BlockSpec(memory_space=pltpu.VMEM)
     dma = pltpu.SemaphoreType.DMA

time: 163 us -> 158 us (0.969)
  the two profiles are of different devices: /device:TPU:0 before, /device:TPU:111 now
where the time goes in v6:
time: 158 us
  Pallas kernels  157 us (99%)
    pallas_call x1, Pallas kernels, body(): pl.pallas_call(functools.partial(kernel, n_sec, n_dp), out_shape=(vmem((t...  154 us
    pallas_call x1, Pallas kernels, body(): pl.pallas_call(store, out_shape=(jax.ShapeDtypeStruct((1, micro, block, w...  3.21 us

profile of v6, /device:TPU:111, one launch (start us, length us, event | category | flops | bytes accessed | tf_op | source)
XLA Modules:
  0.0 158.2 jit_solution(9578589059533497199)
XLA Ops:
  1.3 153.7 %shard_map.130 = (bf16[256,4096]{1,0:T(8,128)(2,1)S(1)}, bf16[256,4096]{1,0:T(8,128)(2,1)S(1)}, f32[2,768,256]{2,1,0:T(8,128)S(1)}, bf16[2,128,4096]{2,1,0:T(8,128)(2,1)S(1)}) custom-call(bf16[2,128,8192]{2,1,0:T(8,128)(2,1)} %bitcast.8, bf16[2,128,4096]{2,1,0:T(8,128)(2,1)} %bitcast.9, bf16[2,128,4096]{2,1,0:T(8,128)(2,1)} %bitcast.10, ...), custom_call_target="tpu_custom_call" | custom-call | tf_op jit(solution)/shard_map/pallas_call | solution.py:702
  155.0 3.2 %shard_map.131 = (bf16[1,2,128,8192]{3,2,1,0:T(8,128)(2,1)}, f32[1,2,768,256]{3,2,1,0:T(8,128)}, bf16[1,2,128,4096]{3,2,1,0:T(8,128)(2,1)}) custom-call(bf16[256,4096]{1,0:T(8,128)(2,1)S(1)} %get-tuple-element.7.inc, bf16[256,4096]{1,0:T(8,128)(2,1)S(1)} %get-tuple-element.8.inc2, f32[2,768,256]{2,1,0:T(8,128)S(1)} %get-tuple-element.9.wts, ...), custom_call_target="tpu_custom_call" | custom-call | tf_op jit(solution)/shard_map/pallas_call | solution.py:758

commit v7 on v6

--- a/solution.py
+++ b/solution.py
@@ -11,6 +11,7 @@
 HEAD_DIM = 128
 LATENTS = 64
 CHUNK = 16
+DIRECT2 = 2
 SPLIT2 = 2
 NORM_ROWS = 16
 TOP_ROWS = 32
@@ -284,7 +285,7 @@
             device_id=(mid_at - 1, me), device_id_type=MESH,
         )
 
-    gate_tanh = jnp.tanh(jnp.broadcast_to(gate_ref[...], (CHUNK, 128)))
+    gate_tanh = jnp.tanh(jnp.full((CHUNK, 128), gate_ref[0], F32))
 
     def chain_step(c, dot_values):
         m = c // per_micro
@@ -327,12 +328,14 @@
             hcols = pl.ds(pl.multiple_of(span + lax.rem(c, SPLIT2) * part2 + h * 128, 128), 128)
             inc2[rows, cols] = (inc2[rows, cols].astype(F32) - b * hid[rows, hcols].astype(F32)).astype(BF16)
 
-        @pl.when(jnp.logical_and(sec > 0, jnp.logical_not(mid)))
+        around = jnp.logical_and(mid, c < n_chunks2 - DIRECT2)
+
+        @pl.when(jnp.logical_and(sec > 0, jnp.logical_not(around)))
         def _():
             relay2(c).start()
 
         if detour:
-            @pl.when(mid)
+            @pl.when(around)
             def _():
                 relay2(c, fwd, n_sec - 1).start()
 
@@ -361,21 +364,30 @@
             return lax.rem(y_at + dy, 4) * 4 + lax.rem(x_lo + dx, 2) * 2 + lax.rem(core + dc, 2)
         return lax.rem(me + 1 + OWNERS * g + i, n_dp)
 
-    def project(m, kinds, g):
+    def project(m, kinds, g, held=False):
         owners = [owner_at(g, i) for i in range(OWNERS)]
-        for kind in kinds:
-            project_compute(m, kind, owners)
+        if not held:
+            for kind in kinds:
+                project_compute(m, kind, owners)
         for i, j in enumerate(owners):
+            crosses = lax.rem(j // 2, 2) != x_lo
+            own = OWNERS * g + i == n_dp - 1
             for kind in kinds:
-                own = OWNERS * g + i == n_dp - 1
-
-                @pl.when(jnp.logical_not(own))
+                if held:
+                    now = crosses
+                elif m == 0:
+                    now = jnp.logical_not(jnp.logical_or(own, jnp.logical_and(crosses, mid)))
+                else:
+                    now = jnp.logical_not(own)
+
+                @pl.when(now)
                 def _():
                     a2a_copy(m, kind, j).start()
 
-                @pl.when(own)
-                def _():
-                    a2a_own(m, kind).start()
+                if not held:
+                    @pl.when(own)
+                    def _():
+                        a2a_own(m, kind).start()
 
     def project_compute(m, kind, owners):
         rows = pl.ds(pl.multiple_of(m * block, block), block)
@@ -434,10 +446,18 @@
     def kv_own(kind):
         return pltpu.make_async_copy(kvs.at[kind, me], kv.at[kind, :, my_cols], loc_sem.at[2, kind])
 
+    chip_steps = ((1, 0), (3, 1), (2, 1), (0, 1), (3, 0), (1, 1), (2, 0), (0, 0))
+
+    def chip_at(k):
+        if n_y != 4:
+            return lax.rem(me // 2 + 1 + k, n_dp // 2)
+        dy, dx = (sum(jnp.where(k == i, step[axis], 0) for i, step in enumerate(chip_steps)) for axis in (0, 1))
+        return lax.rem(y_at + dy, 4) * 2 + lax.rem(x_lo + dx, 2)
+
     def next_rows(kind, send):
         @pl.loop(0, n_dp // 2)
         def _(k):
-            pair = lax.rem(me // 2 + 1 + k, n_dp // 2)
+            pair = chip_at(k)
             at = pl.ds(pl.multiple_of(pair * 2 * block, 2 * block), 2 * block)
             out = dot_nn(nl_all[at, :], wlow[kind]).astype(BF16)
             for i in range(2):
@@ -446,7 +466,7 @@
                 send_rows(kind, k)
 
     def send_rows(kind, k):
-        pair = lax.rem(me // 2 + 1 + k, n_dp // 2)
+        pair = chip_at(k)
 
         @pl.when(k < n_dp // 2 - 1)
         def _():
@@ -539,7 +559,7 @@
 
         project_now = jnp.logical_and(c >= per_micro, c < per_micro + n_dp // OWNERS)
 
-        @pl.when(jnp.logical_and(project_now, jnp.logical_not(mid)))
+        @pl.when(project_now)
         def _():
             project(0, (1, 0), c - per_micro)
 
@@ -547,7 +567,7 @@
     def _():
         @pl.loop(0, n_dp // OWNERS)
         def _(k):
-            project(0, (1, 0), k)
+            project(0, (1, 0), k, True)
 
     for kind in (1, 0):
         @pl.loop(0, n_dp // OWNERS)
@@ -587,6 +607,13 @@
     def _():
         second_steps(0, n_chunks2)
         gather_third()
+        straight = [k for k, step in enumerate(chip_steps) if step[1] == 0] if n_y == 4 else []
+
+        def rows_beside(kind):
+            next_rows(kind, False)
+            for k in straight:
+                send_rows(kind, k)
+
         quarter = n_chunks2 // 4
         forward_steps(0, quarter)
         gather_fourth()
@@ -596,18 +623,19 @@
             lambda: part_grads(1),
             lambda: part_grads(0),
             lambda: update_kind(1),
-            lambda: next_rows(1, False),
+            lambda: rows_beside(1),
             lambda: update_kind(0),
-            lambda: next_rows(0, False),
+            lambda: rows_beside(0),
         ]
-        left = n_chunks2 - 2 * quarter
+        left, groups = n_chunks2 - DIRECT2 - 2 * quarter, len(pieces) + 1
         for i, piece in enumerate(pieces):
-            forward_steps(2 * quarter + i * left // len(pieces), 2 * quarter + (i + 1) * left // len(pieces))
+            forward_steps(2 * quarter + i * left // groups, 2 * quarter + (i + 1) * left // groups)
             piece()
-        for kind in (1, 0):
-            @pl.loop(0, n_dp // 2)
-            def _(k):
-                send_rows(kind, k)
+        forward_steps(2 * quarter + len(pieces) * left // groups, n_chunks2 - DIRECT2)
+        for k in range(n_dp // 2):
+            if k not in straight:
+                for kind in (1, 0):
+                    send_rows(kind, k)
 
     @pl.when(jnp.logical_not(top))
     def _():
@@ -621,7 +649,7 @@
             (gather_end, 0, 13, 15),
             (lambda: part_grads(1), 0, 13, 15),
             (lambda: part_grads(0), 0, 14, 16),
-            (lambda: update_kind(1), jnp.where(sec > 0, 3 + sec, 0), 16, 16),
+            (lambda: update_kind(1), jnp.where(sec > 0, 3 + sec, 0), 15, 16),
             (lambda: next_rows(1, True), jnp.where(sec > 0, 4 + sec, 0), 16, 16),
             (lambda: update_kind(0), jnp.where(sec > 0, 7 + 2 * sec, 0), 16, 16),
             (lambda: next_rows(0, True), jnp.where(sec > 0, 8 + 2 * sec, 0), 16, 16),
@@ -651,7 +679,7 @@
     if detour:
         @pl.when(top)
         def _():
-            @pl.loop(0, n_chunks2)
+            @pl.loop(0, n_chunks2 - DIRECT2)
             def _(c):
                 forward2(c).wait_send()
 
@@ -707,7 +735,7 @@
             vmem((2, lat_w, cols_d), F32),
             vmem((2, rows_m, span), BF16),
         ),
-        in_specs=[any_spec] * 5 + [vmem_spec, any_spec, vmem_spec] + [any_spec] * 3,
+        in_specs=[any_spec] * 5 + [vmem_spec, any_spec, pl.BlockSpec(memory_space=pltpu.SMEM)] + [any_spec] * 3,
         out_specs=(vmem_spec,) * 4,
         scratch_shapes=[
             vmem((tokens, width), BF16),
@@ -753,7 +781,7 @@
         ),
     )(
         hidden_states[0], key_rows[0], value_rows[0], latents, next_latents, media_index, cotangent,
-        gate_alpha.reshape(1, 1), weights[0], moment_first[0], moment_second[0],
+        gate_alpha, weights[0], moment_first[0], moment_second[0],
     )
     grad_in, new_w, kv = pl.pallas_call(
         store,

time: 158 us -> 157 us (level)
  the two profiles are of different devices: /device:TPU:111 before, /device:TPU:0 now
where the time goes in v7:
time: 157 us; the launch traced here: 155 us
  Pallas kernels  154 us (98%)
    pallas_call x1, Pallas kernels, body(): pl.pallas_call(functools.partial(kernel, n_sec, n_dp), out_shape=(vmem((t...  150 us
    pallas_call x1, Pallas kernels, body(): pl.pallas_call(store, out_shape=(jax.ShapeDtypeStruct((1, micro, block, w...  3.21 us

profile of v7, /device:TPU:0, one launch (start us, length us, event | category | flops | bytes accessed | tf_op | source)
XLA Modules:
  0.0 154.9 jit_solution(10133613920857360587)
XLA Ops:
  1.3 150.4 %shard_map.130 = (bf16[256,4096]{1,0:T(8,128)(2,1)S(1)}, bf16[256,4096]{1,0:T(8,128)(2,1)S(1)}, f32[2,768,256]{2,1,0:T(8,128)S(1)}, bf16[2,128,4096]{2,1,0:T(8,128)(2,1)S(1)}) custom-call(bf16[2,128,8192]{2,1,0:T(8,128)(2,1)} %bitcast.6, bf16[2,128,4096]{2,1,0:T(8,128)(2,1)} %bitcast.7, bf16[2,128,4096]{2,1,0:T(8,128)(2,1)} %bitcast.8, ...), custom_call_target="tpu_custom_call" | custom-call | tf_op jit(solution)/shard_map/pallas_call | solution.py:730
  151.7 3.2 %shard_map.131 = (bf16[1,2,128,8192]{3,2,1,0:T(8,128)(2,1)}, f32[1,2,768,256]{3,2,1,0:T(8,128)}, bf16[1,2,128,4096]{3,2,1,0:T(8,128)(2,1)}) custom-call(bf16[256,4096]{1,0:T(8,128)(2,1)S(1)} %get-tuple-element.7.inc, bf16[256,4096]{1,0:T(8,128)(2,1)S(1)} %get-tuple-element.8.inc2, f32[2,768,256]{2,1,0:T(8,128)S(1)} %get-tuple-element.9.wts, ...), custom_call_target="tpu_custom_call" | custom-call | tf_op jit(solution)/shard_map/pallas_call | solution.py:786

commit v8 on v7

--- a/solution.py
+++ b/solution.py
@@ -14,7 +14,7 @@
 DIRECT2 = 2
 SPLIT2 = 2
 NORM_ROWS = 16
-TOP_ROWS = 32
+TOP_ROWS = 16
 OWNERS = 4
 GROUP = 8
 ADAM_ROWS = 64

time: 157 us -> 157 us (level)
  no operation moved by 1% of the time
where the time goes in v8:
time: 157 us; the launch traced here: 155 us
  Pallas kernels  154 us (98%)
    pallas_call x1, Pallas kernels, body(): pl.pallas_call(functools.partial(kernel, n_sec, n_dp), out_shape=(vmem((t...  150 us
    pallas_call x1, Pallas kernels, body(): pl.pallas_call(store, out_shape=(jax.ShapeDtypeStruct((1, micro, block, w...  3.21 us

profile of v8, /device:TPU:0, one launch (start us, length us, event | category | flops | bytes accessed | tf_op | source)
XLA Modules:
  0.0 154.9 jit_solution(4982461024490502073)
XLA Ops:
  1.3 150.4 %shard_map.130 = (bf16[256,4096]{1,0:T(8,128)(2,1)S(1)}, bf16[256,4096]{1,0:T(8,128)(2,1)S(1)}, f32[2,768,256]{2,1,0:T(8,128)S(1)}, bf16[2,128,4096]{2,1,0:T(8,128)(2,1)S(1)}) custom-call(bf16[2,128,8192]{2,1,0:T(8,128)(2,1)} %bitcast.6, bf16[2,128,4096]{2,1,0:T(8,128)(2,1)} %bitcast.7, bf16[2,128,4096]{2,1,0:T(8,128)(2,1)} %bitcast.8, ...), custom_call_target="tpu_custom_call" | custom-call | tf_op jit(solution)/shard_map/pallas_call | solution.py:730
  151.7 3.2 %shard_map.131 = (bf16[1,2,128,8192]{3,2,1,0:T(8,128)(2,1)}, f32[1,2,768,256]{3,2,1,0:T(8,128)}, bf16[1,2,128,4096]{3,2,1,0:T(8,128)(2,1)}) custom-call(bf16[256,4096]{1,0:T(8,128)(2,1)S(1)} %get-tuple-element.7.inc, bf16[256,4096]{1,0:T(8,128)(2,1)S(1)} %get-tuple-element.8.inc2, f32[2,768,256]{2,1,0:T(8,128)S(1)} %get-tuple-element.9.wts, ...), custom_call_target="tpu_custom_call" | custom-call | tf_op jit(solution)/shard_map/pallas_call | solution.py:786
